TPU v7x, 32 devices: a whole 2x2x4 slice. The times are simulated.
32 devices in a mesh: rows: 8 (over z, y), rep: 4 (over x, core).
Axes of the slice: x: 2, y: 2, z: 4, core: 2. Of those that a mesh axis runs over, the one named last changes fastest.
Arguments:
- features: bfloat16 [16384, 128], P('rows')
- weight: bfloat16 [128, 128], replicated, may hold values from -0.5 to 0.5
- bias: float32 [128], replicated, may hold values from -3 to 3
- grad_out: bfloat16 [16384, 128], P('rows')
- tile_values: bfloat16 [8, 4, 128, 64, 64], P('rows', 'rep')
- tile_rows: int32 [8, 4, 128], P('rows', 'rep'), may hold values from 0 to 31
- tile_cols: int32 [8, 4, 128], P('rows', 'rep'), may hold values from 0 to 255, as said below
- tile_count: int32 [8, 4], P('rows', 'rep'), may hold values from 2 to 128, as said below
Outputs:
- hidden: bfloat16 [16384, 128], P('rows')
- grad_w: float32 [128, 128], replicated
- grad_b: float32 [128], replicated
Inputs may be any that keep to these rules, and one draw needn't show every extreme that they name: tile_count is 128 on some device in every draw. tile_cols[i, j, t] // 32 is a row block k with k % 4 == j.
All inputs are finite; a program needn't handle non-finite values.
Results may differ from a plain program's by a relative error of at most 0.007.
Values may be sent and summed in bfloat16 or wider, within the bound.
A program may use at most 64 MiB of HBM per device.

v0:
```python
import jax
import jax.numpy as jnp
from jax import lax
from jax.sharding import PartitionSpec as P


def broadcast(block, axis, source):
    block = jnp.where(lax.axis_index(axis) == source, block, jnp.zeros_like(block))
    return lax.psum(block, axis)


def dense_part(summed, scaled, inv_root, weight, bias, grad_out):
    smoothed = (inv_root[:, None] * (summed + scaled.astype(jnp.float32))).astype(jnp.bfloat16)
    preact = jnp.dot(smoothed, weight, preferred_element_type=jnp.float32) + bias
    hidden = jax.nn.silu(preact).astype(jnp.bfloat16)
    sigmoid_pre = jax.nn.sigmoid(preact)
    silu_slope = sigmoid_pre * (1.0 + preact * (1.0 - sigmoid_pre))
    grad_pre = grad_out.astype(jnp.float32) * silu_slope
    grad_low = grad_pre.astype(jnp.bfloat16)
    grad_w = lax.dot_general(
        smoothed, grad_low, (((0,), (0,)), ((), ())), preferred_element_type=jnp.float32
    )
    return (hidden, grad_w, jnp.sum(grad_pre, axis=0))


def local(features, weight, bias, grad_out, tile_values, tile_rows, tile_cols, tile_count):
    values = tile_values[0, 0]
    row_ids = tile_rows[0, 0]
    col_ids = tile_cols[0, 0]
    live_count = tile_count[0, 0]
    block_len, feat_len = features.shape
    slot_len, tile_len = (values.shape[0], values.shape[1])
    tiles_per_block = block_len // tile_len
    copies = lax.axis_size("rep")
    sections = lax.axis_size("rows") // copies
    replica = lax.axis_index("rep")
    slot_ids = jnp.arange(slot_len, dtype=jnp.int32)
    live_slots = slot_ids < live_count
    row_sums = jnp.where(
        live_slots[:, None], jnp.sum(values, axis=2, dtype=jnp.float32), jnp.float32(0.0)
    )
    local_degree = jnp.zeros((tiles_per_block, tile_len), jnp.float32).at[row_ids].add(row_sums)
    degree = lax.psum(local_degree, "rep")
    inv_root = lax.rsqrt(1.0 + degree.reshape(block_len))
    scaled = (features.astype(jnp.float32) * inv_root[:, None]).astype(jnp.bfloat16)
    panels = []
    for section in range(sections):
        panels.append(broadcast(scaled, "rows", section * copies + replica))
    buffer = jnp.stack(panels).reshape(sections * tiles_per_block, tile_len, feat_len)
    column_block = col_ids // tiles_per_block
    local_index = column_block // copies * tiles_per_block + col_ids % tiles_per_block
    group_len = 64
    passes = (live_count + group_len - 1) // group_len

    def add_group(number, running):
        first_slot = number * group_len
        chosen_values = lax.dynamic_slice_in_dim(values, first_slot, group_len, 0)
        chosen_live = lax.dynamic_slice_in_dim(live_slots, first_slot, group_len, 0)
        chosen_rows = lax.dynamic_slice_in_dim(row_ids, first_slot, group_len, 0)
        chosen_index = lax.dynamic_slice_in_dim(local_index, first_slot, group_len, 0)
        chosen_values = jnp.where(
            chosen_live[:, None, None], chosen_values, jnp.zeros((), chosen_values.dtype)
        )
        products = jnp.einsum(
            "tab,tbf->taf", chosen_values, buffer[chosen_index], preferred_element_type=jnp.float32
        )
        return running.at[chosen_rows].add(products)

    start_sum = jnp.zeros((tiles_per_block, tile_len, feat_len), jnp.float32)
    running = lax.fori_loop(0, passes, add_group, start_sum)
    partial_value = running.reshape(block_len, feat_len)
    summed = lax.psum(partial_value, "rep")
    hidden, grad_w, grad_b = dense_part(summed, scaled, inv_root, weight, bias, grad_out)
    grad_w, grad_b = lax.psum((grad_w, grad_b), "rows")
    return (hidden, grad_w, grad_b)


def solution(mesh):
    return jax.shard_map(
        local,
        mesh=mesh,
        in_specs=(
            P("rows", None),
            P(),
            P(),
            P("rows", None),
            P("rows", "rep", None, None, None),
            P("rows", "rep", None),
            P("rows", "rep", None),
            P("rows", "rep"),
        ),
        out_specs=(P("rows", None), P(), P()),
        check_vma=False,
    )
```

profile of v0, /device:TPU:0, one launch (start us, length us, event | category | flops | bytes accessed | tf_op | source)
XLA Modules:
  0.0 245.1 jit_solution(279571313253590869)
XLA Ops:
  7.2 0.0 copy-start
  7.2 0.0 all-reduce.9.cloned.1.call-start
  7.9 0.7 fusion.15
  8.6 0.0 copy-start.3
  8.6 4.0 %copy.11 = bf16[1,1,128,64,64]{4,3,2,1,0:T(8,128)(2,1)S(1)} copy(bf16[1,1,128,64,64]{2,4,3,1,0:T(8,128)(2,1)} %param.14) | data formatting | bytes 2097152 | tf_op args[4]
  12.6 0.0 copy-start.2
  12.6 0.0 copy-start.6
  12.6 1.2 convert_reduce_fusion
  13.7 1.1 scatter_custom_fusion.1
  14.8 12.7 %psum.42 = f32[32,64]{1,0:T(8,128)S(1)} all-reduce(f32[32,64]{1,0:T(8,128)S(1)} %scatter_custom_fusion.1), channel_id=1, replica_groups=mesh['rows'=8,'rep'=4] {'rep'}, use_global_device_ids=true, to_apply=%region_2.3 | all-reduce | flops 2048 | bytes 16384 | tf_op jit(solution)/shard_map/psum | solution.py:43
  27.5 0.1 rsqrt.11
  27.6 0.0 copy-done.3
  27.6 1.3 select_bitcast_fusion.1
  28.9 0.0 copy-start.4
  28.9 0.0 all-reduce.9.cloned.1.call-update
  28.9 0.0 copy-done.2
  28.9 0.0 all-reduce.5.cloned.1.call-start
  29.0 0.0 copy-done.6
  29.0 78.6 %all-reduce.9.cloned.1.call-done = (bf16[1,2048,128]{2,1,0:T(8,128)(2,1)}, bf16[1,2048,128]{2,1,0:T(8,128)(2,1)}) async-done(((bf16[1,2048,128]{2,1,0:T(8,128)(2,1)}, bf16[1,2048,128]{2,1,0:T(8,128)(2,1)}), (bf16[1,2048,128]{2,1,0:T(8,128)(2,1)}, bf16[1,2048,128]{2,1,0:T(8,128)(2,1)})) %all-reduce.9.cloned.1.call-update) | async-done | bytes 1048592 | tf_op jit(solution)/shard_map/psum | solution.py:9
  107.7 2.3 pad_maximum_fusion
  110.0 0.1 broadcast_in_dim.45
  110.1 0.0 copy-done.4
  110.1 8.8 %while.10 = (s32[]{:T(128)}, f32[32,64,128]{2,1,0:T(8,128)S(1)}, s32[]{:T(128)}, s32[128]{0:T(128)S(1)}, pred[128]{0:T(512)(128)(4,1)S(1)}, /*index=5*/bf16[128,...) while((s32[]{:T(128)}, f32[32,64,128]{2,1,0:T(8,128)S(1)}, ...), condition=%wide.region_7.8_spmd, body=%wide.region_5.7_spmd.sunk | while | flops 67896712 | bytes 12589167 | solution.py:70
  110.1 0.1 dynamic_slice.23
  110.2 0.1 compare_select_fusion.10
  110.3 2.9 %gather_fusion = bf16[64,64,128]{2,1,0:T(8,128)(2,1)} fusion(bf16[64,64,128]{2,1,0:T(8,128)(2,1)} %get-tuple-element.160, s32[1024]{0:T(1024)S(1)} %pad_clamp_fusion.2), kind=kCustom, calls=%fused_computation.clone.1 | custom fusion | bytes 2097408 | tf_op jit(solution)/shard_map/while/body/gather | solution.py:65
  113.1 2.0 fusion.27
  115.2 3.7 %scatter_fusion = f32[32,64,128]{2,1,0:T(8,128)S(1)} fusion(f32[32,64,128]{2,1,0:T(8,128)S(1)} %get-tuple-element.142, s32[64]{0:T(128)S(1)} %get-tuple-element.127, f32[64,64,128]{2,1,0:T(8,128)S(1)} %fusion.27), kind=kCustom, calls=%fused_computation.1.clone.1 | custom fusion | flops 524288 | bytes 6291712 | tf_op jit(solution)/shard_map/while/body/scatter-add | solution.py:67
  118.9 0.0 copy-start.1
  118.9 0.0 copy-start.5
  118.9 0.0 copy-start.7
  118.9 1.0 copy-done.1
  119.9 0.0 all-reduce.5.cloned.1.call-update
  120.0 0.0 all-reduce.7.cloned.1.call-start
  120.0 43.8 %all-reduce.5.cloned.1.call-done = f32[2048,128]{1,0:T(8,128)} async-done(((f32[2048,128]{1,0:T(8,128)}), f32[2048,128]{1,0:T(8,128)}) %all-reduce.5.cloned.1.call-update) | async-done | bytes 1048592 | tf_op jit(solution)/shard_map/psum | solution.py:72
  163.8 1.7 multiply_convert_fusion.1
  165.5 0.0 copy-done
  165.5 0.0 copy-done.5
  165.5 0.0 copy-done.7
  165.5 1.5 fusion.16
  167.0 1.0 fusion.7
  168.0 0.0 all-reduce.7.cloned.1.call-update
  168.0 21.9 %psum.47 = f32[128]{0:T(128)} all-reduce(f32[128]{0:T(128)S(1)} %get-tuple-element.65), channel_id=1, replica_groups=mesh['rows'=8,'rep'=4] {'rows'}, use_global_device_ids=true, to_apply=%region_11.12 | all-reduce | flops 128 | bytes 1024 | tf_op jit(solution)/shard_map/psum | solution.py:74
  189.9 47.1 %all-reduce.7.cloned.1.call-done = f32[128,128]{1,0:T(8,128)} async-done(((f32[128,128]{1,0:T(8,128)}), f32[128,128]{1,0:T(8,128)}) %all-reduce.7.cloned.1.call-update) | async-done | bytes 65552 | tf_op jit(solution)/shard_map/psum | solution.py:74
  237.1 1.5 copy.24
  (4 shorter events, 0.0 us)
Async XLA Ops:
  7.2 158.4 %copy-start = (bf16[128,128]{1,0:T(8,128)(2,1)S(1)}, bf16[128,128]{1,0:T(8,128)(2,1)}, u32[]{:S(2)}) copy-start(bf16[128,128]{1,0:T(8,128)(2,1)} %param.11) | copy-start | bytes 98308
  7.2 100.5 %all-reduce.9.cloned.1.call-start = ((), (), s32[]{:S(2)}) async-start(), calls=%async_computation.2 | async-start | bytes 2097152 | tf_op jit(solution)/shard_map/psum | solution.py:9
  8.6 19.0 %copy-start.3 = (bf16[2048,128]{1,0:T(8,128)(2,1)S(1)}, bf16[2048,128]{1,0:T(8,128)(2,1)}, u32[]{:S(2)}) copy-start(bf16[2048,128]{1,0:T(8,128)(2,1)} %param.10) | copy-start | bytes 1572868
  12.6 16.4 %copy-start.2 = (bf16[1,1,128,64,64]{4,3,2,1,0:T(8,128)(2,1)}, bf16[1,1,128,64,64]{4,3,2,1,0:T(8,128)(2,1)S(1)}, u32[]{:S(2)}) copy-start(bf16[1,1,128,64,64]{4,3,2,1,0:T(8,128)(2,1)S(1)} %copy.11) | copy-start | bytes 3145732
  12.6 16.4 %copy-start.6 = (s32[1,1,128]{2,1,0:T(1,128)S(1)}, s32[1,1,128]{2,1,0:T(1,128)}, u32[]{:S(2)}) copy-start(s32[1,1,128]{2,1,0:T(1,128)} %param.16) | copy-start | bytes 1540
  28.9 81.2 %copy-start.4 = (s32[1,1,128]{2,1,0:T(1,128)S(1)}, s32[1,1,128]{2,1,0:T(1,128)}, u32[]{:S(2)}) copy-start(s32[1,1,128]{2,1,0:T(1,128)} %param.15) | copy-start | bytes 1540
  28.9 134.9 %all-reduce.5.cloned.1.call-start = ((), (), s32[]{:S(2)}) async-start(), calls=%async_computation | async-start | bytes 2097152 | tf_op jit(solution)/shard_map/psum | solution.py:72
  118.9 1.0 copy-start.1
  118.9 46.6 %copy-start.5 = (bf16[2048,128]{1,0:T(8,128)(2,1)S(1)}, bf16[2048,128]{1,0:T(8,128)(2,1)}, u32[]{:S(2)}) copy-start(bf16[2048,128]{1,0:T(8,128)(2,1)} %param.13) | copy-start | bytes 1572868
  118.9 46.6 %copy-start.7 = (f32[128]{0:T(128)S(1)}, f32[128]{0:T(128)}, u32[]{:S(2)}) copy-start(f32[128]{0:T(128)} %param.12) | copy-start | bytes 1540
  120.0 117.1 %all-reduce.7.cloned.1.call-start = ((), (), s32[]{:S(2)}) async-start(), calls=%async_computation.1 | async-start | bytes 131072 | tf_op jit(solution)/shard_map/psum | solution.py:74
Sparse Core Ops, SparseCore 0:
  29.0 78.5 all-reduce.8
  120.1 43.6 all-reduce.4
  168.2 68.8 all-reduce.6
where the time goes:
time: 246 us; the launch traced here: 245 us
  waiting for transfers between devices  170 us (69%)
  blocking collectives  34.5 us (14%)
  between operations  14.6 us (6%)
  other arithmetic  12 us (5%)
  local copies, waits for them, and re-layouts  9.65 us (4%)
  matrix products  4.49 us (2%)
    psum x1, waiting for transfers between devices, broadcast(): return lax.psum(block, axis)  78.6 us
    psum x1, waiting for transfers between devices, local(): grad_w, grad_b = lax.psum((grad_w, grad_b), 'rows')  47.1 us
    psum x1, waiting for transfers between devices, local(): summed = lax.psum(partial_value, 'rep')  43.8 us
    psum x1, blocking collectives, local(): grad_w, grad_b = lax.psum((grad_w, grad_b), 'rows')  21.9 us
    psum x1, blocking collectives, local(): degree = lax.psum(local_degree, 'rep')  12.7 us
    unnamed x18, local copies, waits for them, and re-layouts  6.51 us
  transfers between devices with their start and end apart: 3, of which 3 were waited for; matrix products, arithmetic and copies ran while one was open for 0% of the time, Pallas kernels for 0%

commit v1 on v0

v1 whole, which is shorter than its diff:
```python
import functools
import jax
import jax.numpy as jnp
from jax import lax
from jax.experimental import pallas as pl
from jax.experimental.pallas import tpu as pltpu
from jax.sharding import PartitionSpec as P

MESH = pl.DeviceIdType.MESH
CHUNKS = 4
GROUP = 8


def spread_kernel(R, C, S, feat, ldeg, buf, deg_x, deg_o, send_f, recv_f, send_x, recv_x, send_o, recv_o):
    r = lax.axis_index("rows")
    j = lax.axis_index("rep")
    z = r // 2
    y = r % 2
    Z = R // 2
    rows = feat.shape[0] // CHUNKS

    barrier = pltpu.get_barrier_semaphore()

    def greet(d, carry):
        who = (r * C + j + d) % (R * C)
        pl.semaphore_signal(barrier, inc=1, device_id=(who // C, who % C), device_id_type=MESH)
        return carry

    lax.fori_loop(1, R * C, greet, 0)
    pl.semaphore_wait(barrier, R * C - 1)

    def feature_copy(s, c, way, target, own):
        dst = buf.at[s, pl.ds(c * rows, rows)]
        src = feat.at[pl.ds(c * rows, rows)] if own else dst
        return pltpu.make_async_remote_copy(
            src_ref=src, dst_ref=dst, send_sem=send_f.at[s, c, way], recv_sem=recv_f.at[s, c],
            device_id=(target, j), device_id_type=MESH)

    def ways(s):
        k = s * C + j
        zs = k // 2
        on_column = y == k % 2
        return (
            (0, jnp.logical_and(on_column, jnp.logical_and(z >= zs, z < Z - 1)), r + 2),
            (1, jnp.logical_and(on_column, jnp.logical_and(z <= zs, z > 0)), r - 2),
            (2, on_column, r + 1 - 2 * y),
        )

    for c in range(CHUNKS):
        for s in range(S):
            for way, active, target in ways(s):
                @pl.when(jnp.logical_and(active, r == s * C + j))
                def _():
                    feature_copy(s, c, way, target, True).start()

    home = r % C
    section = r // C

    def degree_copy(d):
        return pltpu.make_async_remote_copy(
            src_ref=ldeg, dst_ref=deg_x.at[section, j], send_sem=send_x.at[d], recv_sem=recv_x.at[section, j],
            device_id=((r + d) % R, home), device_id_type=MESH)

    for d in range(R):
        if d == 0:
            @pl.when(j != home)
            def _():
                degree_copy(0).start()

            @pl.when(j == home)
            def _():
                deg_x[section, j] = ldeg[...]
        else:
            degree_copy(d).start()
    for d in range(1, C):
        pltpu.make_async_remote_copy(
            src_ref=ldeg, dst_ref=deg_o.at[j], send_sem=send_o.at[d], recv_sem=recv_o.at[j],
            device_id=(r, (j + d) % C), device_id_type=MESH).start()
    deg_o[j] = ldeg[...]

    for s in range(S):
        @pl.when(r == s * C + j)
        def _():
            buf[s] = feat[...]

    for c in range(CHUNKS):
        for s in range(S):
            @pl.when(r != s * C + j)
            def _():
                feature_copy(s, c, 0, (r + 1) % R, False).wait_recv()
            for way, active, target in ways(s):
                @pl.when(jnp.logical_and(active, r != s * C + j))
                def _():
                    feature_copy(s, c, way, target, False).start()

    for s in range(S):
        for a in range(C):
            @pl.when(jnp.logical_or(r != s * C + j, a != j))
            def _():
                pltpu.make_async_remote_copy(
                    src_ref=ldeg, dst_ref=deg_x.at[s, a], send_sem=send_x.at[0], recv_sem=recv_x.at[s, a],
                    device_id=((r + 1) % R, j), device_id_type=MESH).wait_recv()
    for d in range(1, C):
        a = (j + d) % C
        copy = pltpu.make_async_remote_copy(
            src_ref=ldeg, dst_ref=deg_o.at[a], send_sem=send_o.at[d], recv_sem=recv_o.at[a],
            device_id=(r, a), device_id_type=MESH)
        copy.wait_recv()
        copy.wait_send()
    for d in range(R):
        if d == 0:
            @pl.when(j != home)
            def _():
                degree_copy(0).wait_send()
        else:
            degree_copy(d).wait_send()
    for c in range(CHUNKS):
        for s in range(S):
            for way, active, target in ways(s):
                @pl.when(active)
                def _():
                    feature_copy(s, c, way, target, False).wait_send()


def tile_kernel(tiles, tile, row_ids, index, count, values, buf, out, total):
    total[...] = jnp.zeros_like(total)
    live = count[0]

    def group(number, carry):
        products = []
        for u in range(GROUP):
            t = number * GROUP + u
            start = pl.multiple_of(index[t] * tile, tile)
            products.append(
                jnp.dot(values[t], buf[pl.ds(start, tile)], preferred_element_type=jnp.float32))
        for u in range(GROUP):
            t = number * GROUP + u
            row = jnp.where(t < live, row_ids[t], tiles)
            place = pl.ds(pl.multiple_of(row * tile, tile), tile)
            total[place] = total[place] + products[u]
        return carry

    lax.fori_loop(0, (live + GROUP - 1) // GROUP, group, 0)
    out[...] = total[: tiles * tile].astype(out.dtype)


def dense_kernel(R, C, part, scaled, inv, grad_out, weight, bias, hidden, grad_w, grad_b,
                 arrived, g1, g1_in, g2_in, low,
                 send_p, recv_p, send_h, recv_h, send_1, recv_1, send_2, recv_2, send_w, recv_w):
    r = lax.axis_index("rows")
    j = lax.axis_index("rep")
    barrier = pltpu.get_barrier_semaphore()
    for d in range(1, C):
        pl.semaphore_signal(barrier, inc=1, device_id=(r, (j + d) % C), device_id_type=MESH)
    for d in range(1, R):
        pl.semaphore_signal(barrier, inc=1, device_id=((r + d) % R, j), device_id_type=MESH)
    pl.semaphore_wait(barrier, R + C - 2)

    def to_rep(d, src, dst, send, recv):
        return pltpu.make_async_remote_copy(
            src_ref=src, dst_ref=dst.at[j], send_sem=send.at[d], recv_sem=recv.at[j],
            device_id=(r, (j + d) % C), device_id_type=MESH)

    def from_rep(d, dst, send, recv):
        a = (j + d) % C
        return pltpu.make_async_remote_copy(
            src_ref=dst.at[a], dst_ref=dst.at[a], send_sem=send.at[d], recv_sem=recv.at[a],
            device_id=(r, a), device_id_type=MESH)

    for d in range(1, C):
        to_rep(d, part.at[(j + d) % C], arrived, send_p, recv_p).start()
    summed = part[j].astype(jnp.float32) + scaled[...].astype(jnp.float32)
    for d in range(1, C):
        from_rep(d, arrived, send_p, recv_p).wait_recv()
        summed = summed + arrived[(j + d) % C].astype(jnp.float32)
    smoothed = (inv[...] * summed).astype(jnp.bfloat16)
    preact = jnp.dot(smoothed, weight[...], preferred_element_type=jnp.float32) + bias[...]
    sig = 1.0 / (1.0 + jnp.exp(-preact))
    hidden[j] = (preact * sig).astype(jnp.bfloat16)
    for d in range(1, C):
        to_rep(d, hidden.at[j], hidden, send_h, recv_h).start()
    grad_pre = grad_out[...].astype(jnp.float32) * (sig * (1.0 + preact * (1.0 - sig)))
    gb = jnp.sum(grad_pre, axis=0, keepdims=True)
    gw = lax.dot_general(smoothed, grad_pre.astype(jnp.bfloat16), (((0,), (0,)), ((), ())),
                         preferred_element_type=jnp.float32)
    share = gw.shape[0] // C
    for a in range(C):
        g1[a, :share] = gw[a * share:(a + 1) * share]
        g1[a, share:] = jnp.broadcast_to(gb, (8, gb.shape[1]))
    for d in range(1, C):
        to_rep(d, g1.at[(j + d) % C], g1_in, send_1, recv_1).start()
    g1_in[j] = g1[j]
    for d in range(1, C):
        from_rep(d, g1_in, send_1, recv_1).wait_recv()
    mine = g1_in[0]
    for a in range(1, C):
        mine = mine + g1_in[a]
    low[...] = mine

    def to_rows(d):
        return pltpu.make_async_remote_copy(
            src_ref=low, dst_ref=g2_in.at[r], send_sem=send_2.at[d], recv_sem=recv_2.at[r],
            device_id=((r + d) % R, j), device_id_type=MESH)

    for d in range(1, R):
        to_rows(d).start()
    g2_in[r] = mine
    for d in range(1, R):
        a = (r + d) % R
        pltpu.make_async_remote_copy(
            src_ref=low, dst_ref=g2_in.at[a], send_sem=send_2.at[d], recv_sem=recv_2.at[a],
            device_id=(a, j), device_id_type=MESH).wait_recv()
    whole = g2_in[0]
    for a in range(1, R):
        whole = whole + g2_in[a]
    grad_w[j] = whole[:share]
    grad_b[...] = whole[share:share + 1]
    for d in range(1, C):
        to_rep(d, grad_w.at[j], grad_w, send_w, recv_w).start()
    for d in range(1, C):
        from_rep(d, grad_w, send_w, recv_w).wait_recv()
        from_rep(d, hidden, send_h, recv_h).wait_recv()
    for d in range(1, C):
        to_rep(d, part.at[(j + d) % C], arrived, send_p, recv_p).wait_send()
        to_rep(d, hidden.at[j], hidden, send_h, recv_h).wait_send()
        to_rep(d, g1.at[(j + d) % C], g1_in, send_1, recv_1).wait_send()
        to_rep(d, grad_w.at[j], grad_w, send_w, recv_w).wait_send()
    for d in range(1, R):
        to_rows(d).wait_send()


def local(features, weight, bias, grad_out, tile_values, tile_rows, tile_cols, tile_count):
    values = tile_values[0, 0]
    row_ids = tile_rows[0, 0]
    col_ids = tile_cols[0, 0]
    live_count = tile_count[0, 0]
    N, F = features.shape
    T, tile = values.shape[0], values.shape[1]
    tiles = N // tile
    R = lax.axis_size("rows")
    C = lax.axis_size("rep")
    S = R // C
    j = lax.axis_index("rep")
    vmem = pl.BlockSpec(memory_space=pltpu.VMEM)
    smem = pl.BlockSpec(memory_space=pltpu.SMEM)
    dma = pltpu.SemaphoreType.DMA
    f32, bf16 = jnp.float32, jnp.bfloat16
    sds = jax.ShapeDtypeStruct

    row_sums = jnp.sum(values, axis=2, dtype=f32)
    place = jnp.logical_and(
        row_ids[None, :] == jnp.arange(tiles, dtype=jnp.int32)[:, None],
        jnp.arange(T, dtype=jnp.int32)[None, :] < live_count)
    local_degree = jnp.dot(place.astype(f32), row_sums, precision=lax.Precision.HIGHEST)
    ldeg = local_degree.reshape(N // 128, 128)

    buf, deg_x, deg_o = pl.pallas_call(
        functools.partial(spread_kernel, R, C, S),
        out_shape=(sds((S, N, F), bf16), sds((S, C, N // 128, 128), f32), sds((C, N // 128, 128), f32)),
        in_specs=[vmem] * 2,
        out_specs=(vmem,) * 3,
        scratch_shapes=[
            dma((S, CHUNKS, 3)), dma((S, CHUNKS)), dma((R,)), dma((S, C)), dma((C,)), dma((C,))],
        compiler_params=pltpu.CompilerParams(
            collective_id=0, has_side_effects=True, vmem_limit_bytes=32 * 2**20),
    )(features, ldeg)

    inv_x = lax.rsqrt(1.0 + jnp.sum(deg_x, axis=1).reshape(S, N))
    scaled_x = (buf.astype(f32) * inv_x[:, :, None]).astype(bf16).reshape(S * N, F)
    inv_o = lax.rsqrt(1.0 + jnp.sum(deg_o, axis=0).reshape(N))
    column_block = col_ids // tiles
    local_index = column_block // C * tiles + col_ids % tiles

    part = pl.pallas_call(
        functools.partial(tile_kernel, tiles, tile),
        out_shape=sds((N, F), bf16),
        in_specs=[smem, smem, smem, vmem, vmem],
        out_specs=vmem,
        scratch_shapes=[pltpu.VMEM(((tiles + 1) * tile, F), f32)],
        compiler_params=pltpu.CompilerParams(vmem_limit_bytes=32 * 2**20),
    )(row_ids, local_index, live_count[None], values, scaled_x)

    q = N // C
    own_inv = jnp.broadcast_to(lax.dynamic_slice_in_dim(inv_o, j * q, q)[:, None], (q, F))
    own_scaled = (lax.dynamic_slice_in_dim(features, j * q, q).astype(f32) * own_inv).astype(bf16)
    own_grad = lax.dynamic_slice_in_dim(grad_out, j * q, q)
    share = F // C
    hidden, grad_w, grad_b = pl.pallas_call(
        functools.partial(dense_kernel, R, C),
        out_shape=(sds((C, q, F), bf16), sds((C, share, F), f32), sds((1, F), f32)),
        in_specs=[vmem] * 6,
        out_specs=(vmem,) * 3,
        scratch_shapes=[
            pltpu.VMEM((C, q, F), bf16),
            pltpu.VMEM((C, share + 8, F), f32),
            pltpu.VMEM((C, share + 8, F), f32),
            pltpu.VMEM((R, share + 8, F), f32),
            pltpu.VMEM((share + 8, F), f32),
            dma((C,)), dma((C,)), dma((C,)), dma((C,)), dma((C,)), dma((C,)), dma((R,)), dma((R,)),
            dma((C,)), dma((C,))],
        compiler_params=pltpu.CompilerParams(
            collective_id=1, has_side_effects=True, vmem_limit_bytes=32 * 2**20),
    )(part.reshape(C, q, F), own_scaled, own_inv, own_grad, weight, bias[None, :])
    return (hidden.reshape(N, F), grad_w.reshape(F, F), grad_b.reshape(F))


def solution(mesh):
    return jax.shard_map(
        local,
        mesh=mesh,
        in_specs=(
            P("rows", None),
            P(),
            P(),
            P("rows", None),
            P("rows", "rep", None, None, None),
            P("rows", "rep", None),
            P("rows", "rep", None),
            P("rows", "rep"),
        ),
        out_specs=(P("rows", None), P(), P()),
        check_vma=False,
    )
```

time: 246 us -> 71.4 us (0.29)
  waiting for transfers between devices: 170 us -> 0 us
  Pallas kernels: 0 us -> 57.3 us
  blocking collectives: 34.5 us -> 0 us
  between operations: 14.6 us -> 1.46 us
  other arithmetic: 12 us -> 4.71 us
  matrix products: 4.49 us -> 0.14 us
    psum x3 -> x0, waiting for transfers between devices: 170 us -> none  [the longest x1 78.6 us: broadcast(): return lax.psum(block, axis)]
    pallas_call x0 -> x3, Pallas kernels: none -> 57.3 us  [the longest x1 34 us: local(): pl.pallas_call(functools.partial(dense_kernel, R, C), out_shape=(sds((C,...]
    psum x2 -> x0, blocking collectives: 34.5 us -> none  [the longest x1 21.9 us: local(): grad_w, grad_b = lax.psum((grad_w, grad_b), 'rows')]
    scatter-add x2 -> x0, other arithmetic: 4.8 us -> none  [the longest x1 3.71 us: add_group(): return running.at[chosen_rows].add(products)]
    dot_general x3 -> x1, matrix products: 4.49 us -> 0.14 us  [local(): jnp.dot(place.astype(f32), row_sums, precision=lax.Precision.HIGHEST)]
    another operation x2 -> x0, other arithmetic: 3.59 us -> none  [local(): jnp.stack(panels).reshape(sections * tiles_per_block, tile_len, feat_len)]
    gather x1 -> x0, local copies, waits for them, and re-layouts: 2.89 us -> none  [add_group(): buffer[chosen_index]]
    unnamed x18 -> x17, local copies, waits for them, and re-layouts: 6.51 us -> 6.96 us
  transfers between devices with their start and end apart: 3 -> 0, of which waited for: 3 -> 0; matrix products, arithmetic and copies ran while one was open for 0% -> 0% of each run, Pallas kernels for 0% -> 0%
where the time goes in v1:
time: 71.4 us; the launch traced here: 70.9 us
  Pallas kernels  57.3 us (80%)
  local copies, waits for them, and re-layouts  7.26 us (10%)
  other arithmetic  4.71 us (7%)
  between operations  1.46 us (2%)
    pallas_call x1, Pallas kernels, local(): pl.pallas_call(functools.partial(dense_kernel, R, C), out_shape=(sds((C,...  34 us
    pallas_call x1, Pallas kernels, local(): pl.pallas_call(functools.partial(spread_kernel, R, C, S), out_shape=(sds(...  22.3 us
    unnamed x17, local copies, waits for them, and re-layouts  6.96 us
    convert_element_type x1, other arithmetic, local(): (buf.astype(f32) * inv_x[:, :, None]).astype(bf16).reshape(S * N, F)  1.76 us

profile of v1, /device:TPU:0, one launch (start us, length us, event | category | flops | bytes accessed | tf_op | source)
XLA Modules:
  0.0 70.9 jit_solution(7032712342277039677)
XLA Ops:
  0.6 0.0 copy-start
  0.6 0.7 %fusion.5.index = s32[128]{0:T(128)S(1)} fusion(s32[1,1,128]{2,1,0:T(1,128)} %param.14), kind=kLoop, calls=%fused_computation.20 | loop fusion | flops 4608 | bytes 1024 | tf_op jit(solution)/shard_map/add | solution.py:272
  2.0 0.0 copy-start.4
  2.0 0.0 copy-start.2
  2.1 4.0 %copy.11 = bf16[1,1,128,64,64]{4,3,2,1,0:T(8,128)(2,1)S(1)} copy(bf16[1,1,128,64,64]{2,4,3,1,0:T(8,128)(2,1)} %param.12) | data formatting | bytes 2097152 | tf_op args[4]
  6.1 1.2 %convert_reduce_fusion = f32[128,64]{1,0:T(8,128)S(1)} fusion(bf16[1,1,128,64,64]{4,3,2,1,0:T(8,128)(2,1)S(1)} %copy.11), kind=kLoop, calls=%fused_computation | loop fusion | flops 1040384 | bytes 1081344 | tf_op jit(solution)/shard_map/reduce_sum | solution.py:250
  7.2 0.0 copy-done.4
  7.2 0.1 fusion.1
  7.4 0.1 reshape.45.ldeg
  7.5 0.0 copy-done.2
  7.5 22.3 %shard_map.103 = (bf16[2,2048,128]{2,1,0:T(8,128)(2,1)S(1)}, f32[2,4,16,128]{3,2,1,0:T(8,128)S(1)}, f32[4,16,128]{2,1,0:T(8,128)S(1)}) custom-call(bf16[2048,128]{1,0:T(8,128)(2,1)S(1)} %copy-done.2, f32[16,128]{1,0:T(8,128)S(1)} %reshape.45.ldeg), custom_call_target="tpu_custom_call" | custom-call | tf_op jit(solution)/shard_map/pallas_call | solution.py:257
  29.7 0.0 copy-start.1
  29.7 1.0 %copy-done.1 = bf16[2,2048,128]{2,1,0:T(8,128)(2,1)} copy-done((bf16[2,2048,128]{2,1,0:T(8,128)(2,1)}, bf16[2,2048,128]{2,1,0:T(8,128)(2,1)S(1)}, u32[]{:S(2)}) %copy-start.1) | copy-done | bytes 1048600
  30.8 1.8 %multiply_convert_fusion = bf16[2,2048,128]{2,1,0:T(8,128)(2,1)S(1)} fusion(bf16[2,2048,128]{2,1,0:T(8,128)(2,1)} %copy-done.1, f32[2,2048]{1,0:T(2,128)S(1)} %bitcast.43), kind=kLoop, calls=%fused_computation.1 | loop fusion | flops 1572864 | bytes 2113536 | tf_op jit(solution)/shard_map/convert_element_type | solution.py:269
  32.5 0.0 copy-start.3
  32.5 0.0 copy-start.5
  32.6 1.0 %shard_map.104 = bf16[2048,128]{1,0:T(8,128)(2,1)S(1)} custom-call(s32[128]{0:T(128)S(1)} %bitcast.40, s32[128]{0:T(128)S(1)} %fusion.5.index, s32[1]{0:T(128)} %bitcast.32.count, bf16[128,64,64]{2,1,0:T(8,128)(2,1)S(1)} %bitcast.34, bf16[4096,128]{1,0:T(8,128)(2,1)S(1)} %bitcast.35), custom_call_target="tpu_custom_call" | custom-call | tf_op jit(solution)/shard_map/pallas_call | solution.py:274
  33.6 0.1 dynamic_slice.10
  33.7 1.0 %multiply_convert_fusion.1.scaled = bf16[512,128]{1,0:T(8,128)(2,1)S(1)} fusion(f32[512]{0:T(512)S(1)} %dynamic_slice.10, bf16[2048,128]{1,0:T(8,128)(2,1)} %feat.1, s32[]{:T(128)S(6)} %select_n.23), kind=kLoop, calls=%fused_computation.2 | loop fusion | flops 196608 | bytes 264196 | tf_op jit(solution)/shard_map/convert_element_type | solution.py:285
  34.8 0.1 broadcast_in_dim.4.inv
  34.9 0.0 copy-done
  34.9 0.0 copy-done.3
  34.9 0.0 copy-done.5
  34.9 34.0 %shard_map.105 = (bf16[4,512,128]{2,1,0:T(8,128)(2,1)S(1)}, f32[4,32,128]{2,1,0:T(8,128)S(1)}, f32[1,128]{1,0:T(1,128)S(1)}) custom-call(bf16[4,512,128]{2,1,0:T(8,128)(2,1)S(1)} %bitcast.36, bf16[512,128]{1,0:T(8,128)(2,1)S(1)} %multiply_convert_fusion.1.scaled, f32[512,128]{1,0:T(8,128)S(1)} %broadcast_in_dim.4.inv, ...), custom_call_target="tpu_custom_call" | custom-call | tf_op jit(solution)/shard_map/pallas_call | solution.py:288
  69.0 0.8 %copy.19 = bf16[2048,128]{1,0:T(8,128)(2,1)} copy(bf16[2048,128]{1,0:T(8,128)(2,1)S(1)} %bitcast.37) | data formatting | bytes 1048576
  69.8 0.6 copy.20
  70.4 0.5 copy.21
  (7 shorter events, 0.1 us)
Async XLA Ops:
  0.6 34.3 %copy-start = (bf16[2048,128]{1,0:T(8,128)(2,1)S(1)}, bf16[2048,128]{1,0:T(8,128)(2,1)}, u32[]{:S(2)}) copy-start(bf16[2048,128]{1,0:T(8,128)(2,1)} %param.11) | copy-start | bytes 1572868
  2.0 5.2 %copy-start.4 = (s32[1,1,128]{2,1,0:T(1,128)S(1)}, s32[1,1,128]{2,1,0:T(1,128)}, u32[]{:S(2)}) copy-start(s32[1,1,128]{2,1,0:T(1,128)} %param.13) | copy-start | bytes 1540
  2.0 5.4 %copy-start.2 = (bf16[2048,128]{1,0:T(8,128)(2,1)S(1)}, bf16[2048,128]{1,0:T(8,128)(2,1)}, u32[]{:S(2)}) copy-start(bf16[2048,128]{1,0:T(8,128)(2,1)} %feat.1) | copy-start | bytes 1572868
  29.7 1.0 %copy-start.1 = (bf16[2,2048,128]{2,1,0:T(8,128)(2,1)}, bf16[2,2048,128]{2,1,0:T(8,128)(2,1)S(1)}, u32[]{:S(2)}) copy-start(bf16[2,2048,128]{2,1,0:T(8,128)(2,1)S(1)} %get-tuple-element.9) | copy-start | bytes 3145732
  32.5 2.4 %copy-start.3 = (bf16[128,128]{1,0:T(8,128)(2,1)S(1)}, bf16[128,128]{1,0:T(8,128)(2,1)}, u32[]{:S(2)}) copy-start(bf16[128,128]{1,0:T(8,128)(2,1)} %weight.1) | copy-start | bytes 98308
  32.5 2.4 %copy-start.5 = (f32[128]{0:T(128)S(1)}, f32[128]{0:T(128)}, u32[]{:S(2)}) copy-start(f32[128]{0:T(128)} %param.10) | copy-start | bytes 1540

commit v2 on v1

--- a/solution.py
+++ b/solution.py
@@ -7,33 +7,40 @@
 from jax.sharding import PartitionSpec as P
 
 MESH = pl.DeviceIdType.MESH
-CHUNKS = 4
+CHUNKS = 16
 GROUP = 8
 
 
-def spread_kernel(R, C, S, feat, ldeg, buf, deg_x, deg_o, send_f, recv_f, send_x, recv_x, send_o, recv_o):
+def spread_kernel(R, C, S, feat, ldeg, buf, deg_x, deg_o, deg_in, send_f, recv_f, send_x, recv_x, send_o, recv_o):
     r = lax.axis_index("rows")
     j = lax.axis_index("rep")
     z = r // 2
     y = r % 2
     Z = R // 2
     rows = feat.shape[0] // CHUNKS
+    neighbours = ((z < Z - 1, r + 2), (z > 0, r - 2))
 
     barrier = pltpu.get_barrier_semaphore()
-
-    def greet(d, carry):
-        who = (r * C + j + d) % (R * C)
-        pl.semaphore_signal(barrier, inc=1, device_id=(who // C, who % C), device_id_type=MESH)
-        return carry
-
-    lax.fori_loop(1, R * C, greet, 0)
-    pl.semaphore_wait(barrier, R * C - 1)
+    for d in range(1, C):
+        pl.semaphore_signal(barrier, inc=1, device_id=(r, (j + d) % C), device_id_type=MESH)
+    pl.semaphore_signal(barrier, inc=1, device_id=(r + 1 - 2 * y, j), device_id_type=MESH)
+    for there, target in neighbours:
+        @pl.when(there)
+        def _():
+            pl.semaphore_signal(barrier, inc=1, device_id=(target, j), device_id_type=MESH)
+    pl.semaphore_wait(barrier, C + jnp.where(z < Z - 1, 1, 0) + jnp.where(z > 0, 1, 0))
 
     def feature_copy(s, c, way, target, own):
-        dst = buf.at[s, pl.ds(c * rows, rows)]
-        src = feat.at[pl.ds(c * rows, rows)] if own else dst
-        return pltpu.make_async_remote_copy(
-            src_ref=src, dst_ref=dst, send_sem=send_f.at[s, c, way], recv_sem=recv_f.at[s, c],
+        place = pl.ds(pl.multiple_of(c * rows, rows), rows)
+        dst = buf.at[s, place]
+        return pltpu.make_async_remote_copy(
+            src_ref=feat.at[place] if own else dst, dst_ref=dst,
+            send_sem=send_f.at[s, c, way], recv_sem=recv_f.at[s, c],
+            device_id=(target, j), device_id_type=MESH)
+
+    def degree_copy(s, way, target):
+        return pltpu.make_async_remote_copy(
+            src_ref=deg_x.at[s], dst_ref=deg_x.at[s], send_sem=send_x.at[s, way], recv_sem=recv_x.at[s],
             device_id=(target, j), device_id_type=MESH)
 
     def ways(s):
@@ -46,80 +53,84 @@
             (2, on_column, r + 1 - 2 * y),
         )
 
-    for c in range(CHUNKS):
-        for s in range(S):
-            for way, active, target in ways(s):
-                @pl.when(jnp.logical_and(active, r == s * C + j))
-                def _():
-                    feature_copy(s, c, way, target, True).start()
-
-    home = r % C
-    section = r // C
-
-    def degree_copy(d):
-        return pltpu.make_async_remote_copy(
-            src_ref=ldeg, dst_ref=deg_x.at[section, j], send_sem=send_x.at[d], recv_sem=recv_x.at[section, j],
-            device_id=((r + d) % R, home), device_id_type=MESH)
-
-    for d in range(R):
-        if d == 0:
-            @pl.when(j != home)
-            def _():
-                degree_copy(0).start()
-
-            @pl.when(j == home)
-            def _():
-                deg_x[section, j] = ldeg[...]
-        else:
-            degree_copy(d).start()
+    def each_chunk(body):
+        def step(c, carry):
+            body(c)
+            return carry
+        lax.fori_loop(0, CHUNKS, step, 0)
+
     for d in range(1, C):
         pltpu.make_async_remote_copy(
-            src_ref=ldeg, dst_ref=deg_o.at[j], send_sem=send_o.at[d], recv_sem=recv_o.at[j],
+            src_ref=ldeg, dst_ref=deg_in.at[j], send_sem=send_o.at[d], recv_sem=recv_o.at[j],
             device_id=(r, (j + d) % C), device_id_type=MESH).start()
-    deg_o[j] = ldeg[...]
 
     for s in range(S):
         @pl.when(r == s * C + j)
         def _():
-            buf[s] = feat[...]
-
-    for c in range(CHUNKS):
-        for s in range(S):
-            @pl.when(r != s * C + j)
-            def _():
-                feature_copy(s, c, 0, (r + 1) % R, False).wait_recv()
-            for way, active, target in ways(s):
-                @pl.when(jnp.logical_and(active, r != s * C + j))
-                def _():
-                    feature_copy(s, c, way, target, False).start()
+            def send_chunk(c):
+                for way, active, target in ways(s):
+                    @pl.when(active)
+                    def _():
+                        feature_copy(s, c, way, target, True).start()
+            each_chunk(send_chunk)
+
+    deg_in[j] = ldeg[...]
+    for d in range(1, C):
+        a = (j + d) % C
+        pltpu.make_async_remote_copy(
+            src_ref=ldeg, dst_ref=deg_in.at[a], send_sem=send_o.at[d], recv_sem=recv_o.at[a],
+            device_id=(r, a), device_id_type=MESH).wait_recv()
+    degree = deg_in[0]
+    for a in range(1, C):
+        degree = degree + deg_in[a]
+    deg_o[...] = degree
 
     for s in range(S):
-        for a in range(C):
-            @pl.when(jnp.logical_or(r != s * C + j, a != j))
-            def _():
-                pltpu.make_async_remote_copy(
-                    src_ref=ldeg, dst_ref=deg_x.at[s, a], send_sem=send_x.at[0], recv_sem=recv_x.at[s, a],
-                    device_id=((r + 1) % R, j), device_id_type=MESH).wait_recv()
-    for d in range(1, C):
-        a = (j + d) % C
-        copy = pltpu.make_async_remote_copy(
-            src_ref=ldeg, dst_ref=deg_o.at[a], send_sem=send_o.at[d], recv_sem=recv_o.at[a],
-            device_id=(r, a), device_id_type=MESH)
-        copy.wait_recv()
-        copy.wait_send()
-    for d in range(R):
-        if d == 0:
-            @pl.when(j != home)
-            def _():
-                degree_copy(0).wait_send()
-        else:
-            degree_copy(d).wait_send()
-    for c in range(CHUNKS):
-        for s in range(S):
+        @pl.when(r == s * C + j)
+        def _():
+            deg_x[s] = degree
             for way, active, target in ways(s):
                 @pl.when(active)
                 def _():
-                    feature_copy(s, c, way, target, False).wait_send()
+                    degree_copy(s, way, target).start()
+            buf[s] = feat[...]
+
+    gaps = [jnp.abs(z - (s * C + j) // 2) for s in range(S)]
+    ranks = []
+    for s in range(S):
+        rank = 0
+        for t in range(S):
+            if t != s:
+                ahead = gaps[t] <= gaps[s] if t < s else gaps[t] < gaps[s]
+                rank = rank + jnp.where(ahead, 1, 0)
+        ranks.append(rank)
+    for i in range(S):
+        for s in range(S):
+            @pl.when(jnp.logical_and(ranks[s] == i, r != s * C + j))
+            def _():
+                def pass_chunk(c):
+                    feature_copy(s, c, 0, r + 1 - 2 * y, False).wait_recv()
+                    for way, active, target in ways(s):
+                        @pl.when(active)
+                        def _():
+                            feature_copy(s, c, way, target, False).start()
+                each_chunk(pass_chunk)
+                degree_copy(s, 0, r + 1 - 2 * y).wait_recv()
+                for way, active, target in ways(s):
+                    @pl.when(active)
+                    def _():
+                        degree_copy(s, way, target).start()
+
+    for d in range(1, C):
+        pltpu.make_async_remote_copy(
+            src_ref=ldeg, dst_ref=deg_in.at[j], send_sem=send_o.at[d], recv_sem=recv_o.at[j],
+            device_id=(r, (j + d) % C), device_id_type=MESH).wait_send()
+    for s in range(S):
+        for way, active, target in ways(s):
+            @pl.when(active)
+            def _():
+                each_chunk(lambda c: feature_copy(s, c, way, target, False).wait_send())
+                degree_copy(s, way, target).wait_send()
 
 
 def tile_kernel(tiles, tile, row_ids, index, count, values, buf, out, total):
@@ -177,8 +188,6 @@
     preact = jnp.dot(smoothed, weight[...], preferred_element_type=jnp.float32) + bias[...]
     sig = 1.0 / (1.0 + jnp.exp(-preact))
     hidden[j] = (preact * sig).astype(jnp.bfloat16)
-    for d in range(1, C):
-        to_rep(d, hidden.at[j], hidden, send_h, recv_h).start()
     grad_pre = grad_out[...].astype(jnp.float32) * (sig * (1.0 + preact * (1.0 - sig)))
     gb = jnp.sum(grad_pre, axis=0, keepdims=True)
     gw = lax.dot_general(smoothed, grad_pre.astype(jnp.bfloat16), (((0,), (0,)), ((), ())),
@@ -189,6 +198,8 @@
         g1[a, share:] = jnp.broadcast_to(gb, (8, gb.shape[1]))
     for d in range(1, C):
         to_rep(d, g1.at[(j + d) % C], g1_in, send_1, recv_1).start()
+    for d in range(1, C):
+        to_rep(d, hidden.at[j], hidden, send_h, recv_h).start()
     g1_in[j] = g1[j]
     for d in range(1, C):
         from_rep(d, g1_in, send_1, recv_1).wait_recv()
@@ -256,18 +267,19 @@
 
     buf, deg_x, deg_o = pl.pallas_call(
         functools.partial(spread_kernel, R, C, S),
-        out_shape=(sds((S, N, F), bf16), sds((S, C, N // 128, 128), f32), sds((C, N // 128, 128), f32)),
+        out_shape=(sds((S, N, F), bf16), sds((S, N // 128, 128), f32), sds((N // 128, 128), f32)),
         in_specs=[vmem] * 2,
         out_specs=(vmem,) * 3,
         scratch_shapes=[
-            dma((S, CHUNKS, 3)), dma((S, CHUNKS)), dma((R,)), dma((S, C)), dma((C,)), dma((C,))],
+            pltpu.VMEM((C, N // 128, 128), f32),
+            dma((S, CHUNKS, 3)), dma((S, CHUNKS)), dma((S, 3)), dma((S,)), dma((C,)), dma((C,))],
         compiler_params=pltpu.CompilerParams(
             collective_id=0, has_side_effects=True, vmem_limit_bytes=32 * 2**20),
     )(features, ldeg)
 
-    inv_x = lax.rsqrt(1.0 + jnp.sum(deg_x, axis=1).reshape(S, N))
+    inv_x = lax.rsqrt(1.0 + deg_x.reshape(S, N))
     scaled_x = (buf.astype(f32) * inv_x[:, :, None]).astype(bf16).reshape(S * N, F)
-    inv_o = lax.rsqrt(1.0 + jnp.sum(deg_o, axis=0).reshape(N))
+    inv_o = lax.rsqrt(1.0 + deg_o.reshape(N))
     column_block = col_ids // tiles
     local_index = column_block // C * tiles + col_ids % tiles
 

time: 71.4 us -> 62.1 us (0.87)
  Pallas kernels: 57.3 us -> 50.3 us
  other arithmetic: 4.71 us -> 3.64 us
  local copies, waits for them, and re-layouts: 7.26 us -> 6.27 us
    pallas_call x1, Pallas kernels: 34 us -> 26.4 us  [local(): pl.pallas_call(functools.partial(dense_kernel, R, C), out_shape=(sds((C,...]
    convert_element_type x1, other arithmetic: 1.76 us -> 0.71 us  [local(): (buf.astype(f32) * inv_x[:, :, None]).astype(bf16).reshape(S * N, F)]
    unnamed x17 -> x15, local copies, waits for them, and re-layouts: 6.96 us -> 5.98 us
where the time goes in v2:
time: 62.1 us; the launch traced here: 61.8 us
  Pallas kernels  50.3 us (81%)
  local copies, waits for them, and re-layouts  6.27 us (10%)
  other arithmetic  3.64 us (6%)
  between operations  1.46 us (2%)
    pallas_call x1, Pallas kernels, local(): pl.pallas_call(functools.partial(dense_kernel, R, C), out_shape=(sds((C,...  26.4 us
    pallas_call x1, Pallas kernels, local(): pl.pallas_call(functools.partial(spread_kernel, R, C, S), out_shape=(sds(...  22.4 us
    unnamed x15, local copies, waits for them, and re-layouts  5.98 us
    pallas_call x1, Pallas kernels, local(): pl.pallas_call(functools.partial(tile_kernel, tiles, tile), out_shape=sds...  1.42 us

profile of v2, /device:TPU:0, one launch (start us, length us, event | category | flops | bytes accessed | tf_op | source)
XLA Modules:
  0.0 61.8 jit_solution(14620911824163039243)
XLA Ops:
  0.6 0.0 copy-start
  0.6 0.7 %fusion.5.index = s32[128]{0:T(128)S(1)} fusion(s32[1,1,128]{2,1,0:T(1,128)} %param.14), kind=kLoop, calls=%fused_computation.20 | loop fusion | flops 4608 | bytes 1024 | tf_op jit(solution)/shard_map/add | solution.py:284
  2.0 0.0 copy-start.3
  2.0 0.0 copy-start.1
  2.1 4.0 %copy.11 = bf16[1,1,128,64,64]{4,3,2,1,0:T(8,128)(2,1)S(1)} copy(bf16[1,1,128,64,64]{2,4,3,1,0:T(8,128)(2,1)} %param.12) | data formatting | bytes 2097152 | tf_op args[4]
  6.1 1.2 %convert_reduce_fusion = f32[128,64]{1,0:T(8,128)S(1)} fusion(bf16[1,1,128,64,64]{4,3,2,1,0:T(8,128)(2,1)S(1)} %copy.11), kind=kLoop, calls=%fused_computation | loop fusion | flops 1040384 | bytes 1081344 | tf_op jit(solution)/shard_map/reduce_sum | solution.py:261
  7.2 0.0 copy-done.3
  7.2 0.1 fusion.1
  7.4 0.1 reshape.45.ldeg
  7.5 0.0 copy-done.1
  7.5 22.4 %shard_map.103 = (bf16[2,2048,128]{2,1,0:T(8,128)(2,1)S(1)}, f32[2,16,128]{2,1,0:T(8,128)S(1)}, f32[16,128]{1,0:T(8,128)S(1)}) custom-call(bf16[2048,128]{1,0:T(8,128)(2,1)S(1)} %copy-done.1, f32[16,128]{1,0:T(8,128)S(1)} %reshape.45.ldeg), custom_call_target="tpu_custom_call" | custom-call | tf_op jit(solution)/shard_map/pallas_call | solution.py:268
  29.9 0.7 %multiply_convert_fusion = bf16[2,2048,128]{2,1,0:T(8,128)(2,1)S(1)} fusion(bf16[2,2048,128]{2,1,0:T(8,128)(2,1)S(1)} %get-tuple-element.9, f32[2,2048]{1,0:T(2,128)S(1)} %bitcast.43), kind=kLoop, calls=%fused_computation.1 | loop fusion | flops 1572864 | bytes 2113536 | tf_op jit(solution)/shard_map/convert_element_type | solution.py:281
  30.6 0.0 copy-start.2
  30.7 0.0 copy-start.4
  30.7 1.4 %shard_map.104 = bf16[2048,128]{1,0:T(8,128)(2,1)S(1)} custom-call(s32[128]{0:T(128)S(1)} %bitcast.40, s32[128]{0:T(128)S(1)} %fusion.5.index, s32[1]{0:T(128)} %bitcast.32.count, bf16[128,64,64]{2,1,0:T(8,128)(2,1)S(1)} %bitcast.34, bf16[4096,128]{1,0:T(8,128)(2,1)S(1)} %bitcast.35), custom_call_target="tpu_custom_call" | custom-call | tf_op jit(solution)/shard_map/pallas_call | solution.py:286
  32.1 0.1 dynamic_slice.10
  32.2 1.0 %multiply_convert_fusion.1.scaled = bf16[512,128]{1,0:T(8,128)(2,1)S(1)} fusion(f32[512]{0:T(512)S(1)} %dynamic_slice.10, bf16[2048,128]{1,0:T(8,128)(2,1)} %feat.1, s32[]{:T(128)S(6)} %select_n.23), kind=kLoop, calls=%fused_computation.2 | loop fusion | flops 196608 | bytes 264196 | tf_op jit(solution)/shard_map/convert_element_type | solution.py:297
  33.2 0.1 broadcast_in_dim.4.inv
  33.4 0.0 copy-done
  33.4 0.0 copy-done.2
  33.4 0.0 copy-done.4
  33.4 26.4 %shard_map.105 = (bf16[4,512,128]{2,1,0:T(8,128)(2,1)S(1)}, f32[4,32,128]{2,1,0:T(8,128)S(1)}, f32[1,128]{1,0:T(1,128)S(1)}) custom-call(bf16[4,512,128]{2,1,0:T(8,128)(2,1)S(1)} %bitcast.36, bf16[512,128]{1,0:T(8,128)(2,1)S(1)} %multiply_convert_fusion.1.scaled, f32[512,128]{1,0:T(8,128)S(1)} %broadcast_in_dim.4.inv, ...), custom_call_target="tpu_custom_call" | custom-call | tf_op jit(solution)/shard_map/pallas_call | solution.py:300
  59.8 0.8 %copy.19 = bf16[2048,128]{1,0:T(8,128)(2,1)} copy(bf16[2048,128]{1,0:T(8,128)(2,1)S(1)} %bitcast.37) | data formatting | bytes 1048576
  60.6 0.6 %copy.20 = f32[128,128]{1,0:T(8,128)} copy(f32[128,128]{1,0:T(8,128)S(1)} %bitcast.38) | data formatting | bytes 131072
  61.3 0.5 copy.21
  (5 shorter events, 0.0 us)
Async XLA Ops:
  0.6 32.7 %copy-start = (bf16[2048,128]{1,0:T(8,128)(2,1)S(1)}, bf16[2048,128]{1,0:T(8,128)(2,1)}, u32[]{:S(2)}) copy-start(bf16[2048,128]{1,0:T(8,128)(2,1)} %param.11) | copy-start | bytes 1572868
  2.0 5.2 %copy-start.3 = (s32[1,1,128]{2,1,0:T(1,128)S(1)}, s32[1,1,128]{2,1,0:T(1,128)}, u32[]{:S(2)}) copy-start(s32[1,1,128]{2,1,0:T(1,128)} %param.13) | copy-start | bytes 1540
  2.0 5.4 %copy-start.1 = (bf16[2048,128]{1,0:T(8,128)(2,1)S(1)}, bf16[2048,128]{1,0:T(8,128)(2,1)}, u32[]{:S(2)}) copy-start(bf16[2048,128]{1,0:T(8,128)(2,1)} %feat.1) | copy-start | bytes 1572868
  30.6 2.8 %copy-start.2 = (bf16[128,128]{1,0:T(8,128)(2,1)S(1)}, bf16[128,128]{1,0:T(8,128)(2,1)}, u32[]{:S(2)}) copy-start(bf16[128,128]{1,0:T(8,128)(2,1)} %weight.1) | copy-start | bytes 98308
  30.7 2.8 %copy-start.4 = (f32[128]{0:T(128)S(1)}, f32[128]{0:T(128)}, u32[]{:S(2)}) copy-start(f32[128]{0:T(128)} %param.10) | copy-start | bytes 1540

commit v3 on v2

--- a/solution.py
+++ b/solution.py
@@ -11,7 +11,7 @@
 GROUP = 8
 
 
-def spread_kernel(R, C, S, feat, ldeg, buf, deg_x, deg_o, deg_in, send_f, recv_f, send_x, recv_x, send_o, recv_o):
+def spread_kernel(R, C, S, feat, stored, row_ids, live, buf, deg_x, deg_o, turned, values, fetched, deg_in, ldeg, send_f, recv_f, send_x, recv_x, send_o, recv_o):
     r = lax.axis_index("rows")
     j = lax.axis_index("rep")
     z = r // 2
@@ -20,6 +20,8 @@
     rows = feat.shape[0] // CHUNKS
     neighbours = ((z < Z - 1, r + 2), (z > 0, r - 2))
 
+    fetch = pltpu.make_async_copy(stored, values, fetched.at[0])
+    fetch.start()
     barrier = pltpu.get_barrier_semaphore()
     for d in range(1, C):
         pl.semaphore_signal(barrier, inc=1, device_id=(r, (j + d) % C), device_id_type=MESH)
@@ -59,11 +61,6 @@
             return carry
         lax.fori_loop(0, CHUNKS, step, 0)
 
-    for d in range(1, C):
-        pltpu.make_async_remote_copy(
-            src_ref=ldeg, dst_ref=deg_in.at[j], send_sem=send_o.at[d], recv_sem=recv_o.at[j],
-            device_id=(r, (j + d) % C), device_id_type=MESH).start()
-
     for s in range(S):
         @pl.when(r == s * C + j)
         def _():
@@ -74,6 +71,23 @@
                         feature_copy(s, c, way, target, True).start()
             each_chunk(send_chunk)
 
+    tile, _, slots = values.shape
+    half = tile // 2
+    fetch.wait()
+    sums = jnp.sum(values[...].astype(jnp.float32), axis=1)
+    shape = (ldeg.shape[0], slots)
+    row = lax.broadcasted_iota(jnp.int32, shape, 0)
+    slot = lax.broadcasted_iota(jnp.int32, shape, 1)
+    place = jnp.where(jnp.logical_and(row_ids[...] == row, slot < live[...]), 1.0, 0.0)
+    ldeg[...] = lax.dot_general(
+        place, sums, (((1,), (1,)), ((), ())),
+        precision=lax.Precision.HIGHEST, preferred_element_type=jnp.float32)
+
+    for d in range(1, C):
+        pltpu.make_async_remote_copy(
+            src_ref=ldeg, dst_ref=deg_in.at[j], send_sem=send_o.at[d], recv_sem=recv_o.at[j],
+            device_id=(r, (j + d) % C), device_id_type=MESH).start()
+
     deg_in[j] = ldeg[...]
     for d in range(1, C):
         a = (j + d) % C
@@ -93,7 +107,20 @@
                 @pl.when(active)
                 def _():
                     degree_copy(s, way, target).start()
-            buf[s] = feat[...]
+            keep = pltpu.make_async_copy(feat, buf.at[s], fetched.at[1])
+            keep.start()
+            keep.wait()
+
+    per = -(-half // (S * CHUNKS))
+
+    def turn(step):
+        for u in range(per):
+            a = step * per + u
+
+            @pl.when(a < half)
+            def _():
+                pair = jnp.concatenate([values[a], values[a + half]], axis=0).astype(jnp.float32)
+                turned[pl.ds(a, slots, stride=half), :] = pair.T
 
     gaps = [jnp.abs(z - (s * C + j) // 2) for s in range(S)]
     ranks = []
@@ -106,9 +133,14 @@
         ranks.append(rank)
     for i in range(S):
         for s in range(S):
+            @pl.when(jnp.logical_and(ranks[s] == i, r == s * C + j))
+            def _():
+                each_chunk(lambda c: turn(i * CHUNKS + c))
+
             @pl.when(jnp.logical_and(ranks[s] == i, r != s * C + j))
             def _():
                 def pass_chunk(c):
+                    turn(i * CHUNKS + c)
                     feature_copy(s, c, 0, r + 1 - 2 * y, False).wait_recv()
                     for way, active, target in ways(s):
                         @pl.when(active)
@@ -133,20 +165,32 @@
                 degree_copy(s, way, target).wait_send()
 
 
-def tile_kernel(tiles, tile, row_ids, index, count, values, buf, out, total):
+def tile_kernel(C, tiles, tile, row_ids, columns, count, values, raw, degree, out, total, buf):
     total[...] = jnp.zeros_like(total)
-    live = count[0]
+    live = count[0, 0]
+    half = tile // 2
+    sections = raw.shape[0]
+    for s in range(sections):
+        inv = lax.rsqrt(1.0 + degree[s].T)
+        for a in range(tiles):
+            block = raw[s, a * tile:(a + 1) * tile].astype(jnp.float32) * inv[:, a:a + 1]
+            start = (s * tiles + a) * tile
+            buf[start:start + tile] = block.astype(buf.dtype)
 
     def group(number, carry):
         products = []
         for u in range(GROUP):
             t = number * GROUP + u
-            start = pl.multiple_of(index[t] * tile, tile)
+            column = columns[0, t]
+            block_index = lax.div(lax.div(column, tiles), C) * tiles + lax.rem(column, tiles)
+            start = pl.multiple_of(block_index * tile, tile)
+            pair = values[pl.ds(pl.multiple_of(t * half, half), half)]
+            block = jnp.concatenate([pair[:, :tile], pair[:, tile:]], axis=0).astype(jnp.bfloat16)
             products.append(
-                jnp.dot(values[t], buf[pl.ds(start, tile)], preferred_element_type=jnp.float32))
+                jnp.dot(block, buf[pl.ds(start, tile)], preferred_element_type=jnp.float32))
         for u in range(GROUP):
             t = number * GROUP + u
-            row = jnp.where(t < live, row_ids[t], tiles)
+            row = jnp.where(t < live, row_ids[0, t], tiles)
             place = pl.ds(pl.multiple_of(row * tile, tile), tile)
             total[place] = total[place] + products[u]
         return carry
@@ -155,7 +199,7 @@
     out[...] = total[: tiles * tile].astype(out.dtype)
 
 
-def dense_kernel(R, C, part, scaled, inv, grad_out, weight, bias, hidden, grad_w, grad_b,
+def dense_kernel(R, C, part, features, degree, grad_out, weight, bias, hidden, grad_w, grad_b,
                  arrived, g1, g1_in, g2_in, low,
                  send_p, recv_p, send_h, recv_h, send_1, recv_1, send_2, recv_2, send_w, recv_w):
     r = lax.axis_index("rows")
@@ -180,15 +224,25 @@
 
     for d in range(1, C):
         to_rep(d, part.at[(j + d) % C], arrived, send_p, recv_p).start()
-    summed = part[j].astype(jnp.float32) + scaled[...].astype(jnp.float32)
+    q, feat_len = part.shape[1:]
+    tile = degree.shape[1]
+    mine_rows = pl.ds(pl.multiple_of(j * q, q), q)
+    roots = lax.rsqrt(1.0 + degree[...].T)
+    lane = lax.broadcasted_iota(jnp.int32, roots.shape, 1)
+    inv = jnp.concatenate([
+        jnp.broadcast_to(
+            jnp.sum(jnp.where(lane == j * (q // tile) + a, roots, 0.0), axis=1, keepdims=True), (tile, feat_len))
+        for a in range(q // tile)], axis=0)
+    scaled = (features[mine_rows].astype(jnp.float32) * inv).astype(jnp.bfloat16)
+    summed = part[j].astype(jnp.float32) + scaled.astype(jnp.float32)
     for d in range(1, C):
         from_rep(d, arrived, send_p, recv_p).wait_recv()
         summed = summed + arrived[(j + d) % C].astype(jnp.float32)
-    smoothed = (inv[...] * summed).astype(jnp.bfloat16)
+    smoothed = (inv * summed).astype(jnp.bfloat16)
     preact = jnp.dot(smoothed, weight[...], preferred_element_type=jnp.float32) + bias[...]
     sig = 1.0 / (1.0 + jnp.exp(-preact))
     hidden[j] = (preact * sig).astype(jnp.bfloat16)
-    grad_pre = grad_out[...].astype(jnp.float32) * (sig * (1.0 + preact * (1.0 - sig)))
+    grad_pre = grad_out[mine_rows].astype(jnp.float32) * (sig * (1.0 + preact * (1.0 - sig)))
     gb = jnp.sum(grad_pre, axis=0, keepdims=True)
     gw = lax.dot_general(smoothed, grad_pre.astype(jnp.bfloat16), (((0,), (0,)), ((), ())),
                          preferred_element_type=jnp.float32)
@@ -242,60 +296,43 @@
 
 def local(features, weight, bias, grad_out, tile_values, tile_rows, tile_cols, tile_count):
     values = tile_values[0, 0]
-    row_ids = tile_rows[0, 0]
-    col_ids = tile_cols[0, 0]
-    live_count = tile_count[0, 0]
     N, F = features.shape
     T, tile = values.shape[0], values.shape[1]
     tiles = N // tile
     R = lax.axis_size("rows")
     C = lax.axis_size("rep")
     S = R // C
-    j = lax.axis_index("rep")
     vmem = pl.BlockSpec(memory_space=pltpu.VMEM)
+    anywhere = pl.BlockSpec(memory_space=pltpu.HBM)
     smem = pl.BlockSpec(memory_space=pltpu.SMEM)
     dma = pltpu.SemaphoreType.DMA
     f32, bf16 = jnp.float32, jnp.bfloat16
     sds = jax.ShapeDtypeStruct
 
-    row_sums = jnp.sum(values, axis=2, dtype=f32)
-    place = jnp.logical_and(
-        row_ids[None, :] == jnp.arange(tiles, dtype=jnp.int32)[:, None],
-        jnp.arange(T, dtype=jnp.int32)[None, :] < live_count)
-    local_degree = jnp.dot(place.astype(f32), row_sums, precision=lax.Precision.HIGHEST)
-    ldeg = local_degree.reshape(N // 128, 128)
-
-    buf, deg_x, deg_o = pl.pallas_call(
+    buf, deg_x, deg_o, turned = pl.pallas_call(
         functools.partial(spread_kernel, R, C, S),
-        out_shape=(sds((S, N, F), bf16), sds((S, N // 128, 128), f32), sds((N // 128, 128), f32)),
-        in_specs=[vmem] * 2,
-        out_specs=(vmem,) * 3,
+        out_shape=(sds((S, N, F), bf16), sds((S, tiles, tile), f32), sds((tiles, tile), f32),
+                   sds((T * tile // 2, 2 * tile), f32)),
+        in_specs=[anywhere, anywhere, vmem, vmem],
+        out_specs=(vmem,) * 4,
         scratch_shapes=[
-            pltpu.VMEM((C, N // 128, 128), f32),
+            pltpu.VMEM((tile, tile, T), bf16), dma((2,)),
+            pltpu.VMEM((C, tiles, tile), f32), pltpu.VMEM((tiles, tile), f32),
             dma((S, CHUNKS, 3)), dma((S, CHUNKS)), dma((S, 3)), dma((S,)), dma((C,)), dma((C,))],
         compiler_params=pltpu.CompilerParams(
             collective_id=0, has_side_effects=True, vmem_limit_bytes=32 * 2**20),
-    )(features, ldeg)
-
-    inv_x = lax.rsqrt(1.0 + deg_x.reshape(S, N))
-    scaled_x = (buf.astype(f32) * inv_x[:, :, None]).astype(bf16).reshape(S * N, F)
-    inv_o = lax.rsqrt(1.0 + deg_o.reshape(N))
-    column_block = col_ids // tiles
-    local_index = column_block // C * tiles + col_ids % tiles
+    )(features, jnp.transpose(values, (1, 2, 0)), tile_rows[0], tile_count)
 
     part = pl.pallas_call(
-        functools.partial(tile_kernel, tiles, tile),
+        functools.partial(tile_kernel, C, tiles, tile),
         out_shape=sds((N, F), bf16),
-        in_specs=[smem, smem, smem, vmem, vmem],
+        in_specs=[smem, smem, smem, vmem, vmem, vmem],
         out_specs=vmem,
-        scratch_shapes=[pltpu.VMEM(((tiles + 1) * tile, F), f32)],
+        scratch_shapes=[pltpu.VMEM(((tiles + 1) * tile, F), f32), pltpu.VMEM((S * N, F), bf16)],
         compiler_params=pltpu.CompilerParams(vmem_limit_bytes=32 * 2**20),
-    )(row_ids, local_index, live_count[None], values, scaled_x)
+    )(tile_rows[0], tile_cols[0], tile_count, turned, buf, deg_x)
 
     q = N // C
-    own_inv = jnp.broadcast_to(lax.dynamic_slice_in_dim(inv_o, j * q, q)[:, None], (q, F))
-    own_scaled = (lax.dynamic_slice_in_dim(features, j * q, q).astype(f32) * own_inv).astype(bf16)
-    own_grad = lax.dynamic_slice_in_dim(grad_out, j * q, q)
     share = F // C
     hidden, grad_w, grad_b = pl.pallas_call(
         functools.partial(dense_kernel, R, C),
@@ -312,7 +349,7 @@
             dma((C,)), dma((C,))],
         compiler_params=pltpu.CompilerParams(
             collective_id=1, has_side_effects=True, vmem_limit_bytes=32 * 2**20),
-    )(part.reshape(C, q, F), own_scaled, own_inv, own_grad, weight, bias[None, :])
+    )(part.reshape(C, q, F), features, deg_o, grad_out, weight, bias[None, :])
     return (hidden.reshape(N, F), grad_w.reshape(F, F), grad_b.reshape(F))
 
 

time: 62.1 us -> 59.8 us (0.963)
  other arithmetic: 3.64 us -> 0 us
  Pallas kernels: 50.3 us -> 52.7 us
  local copies, waits for them, and re-layouts: 6.27 us -> 5.61 us
    convert_element_type x2 -> x0, other arithmetic: 1.74 us -> none  [the longest x1 1.03 us: local(): (lax.dynamic_slice_in_dim(features, j * q, q).astype(f32) * own_inv).asty...]
    pallas_call x1, Pallas kernels: 1.42 us -> 2.67 us  [local(): pl.pallas_call(functools.partial(tile_kernel, C, tiles, tile), out_shape=...]
    reduce_sum x1 -> x0, other arithmetic: 1.15 us -> none  [local(): row_sums = jnp.sum(values, axis=2, dtype=f32)]
    pallas_call x1, Pallas kernels: 26.4 us -> 27.2 us  [local(): pl.pallas_call(functools.partial(dense_kernel, R, C), out_shape=(sds((C,...]
    add x1 -> x0, other arithmetic: 0.73 us -> none  [local(): local_index = column_block // C * tiles + col_ids % tiles]
    unnamed x15 -> x19, local copies, waits for them, and re-layouts: 5.98 us -> 5.61 us
where the time goes in v3:
time: 59.8 us; the launch traced here: 59.7 us
  Pallas kernels  52.7 us (88%)
  local copies, waits for them, and re-layouts  5.61 us (9%)
  between operations  1.38 us (2%)
    pallas_call x1, Pallas kernels, local(): pl.pallas_call(functools.partial(dense_kernel, R, C), out_shape=(sds((C,...  27.2 us
    pallas_call x1, Pallas kernels, local(): pl.pallas_call(functools.partial(spread_kernel, R, C, S), out_shape=(sds(...  22.8 us
    unnamed x19, local copies, waits for them, and re-layouts  5.61 us
    pallas_call x1, Pallas kernels, local(): pl.pallas_call(functools.partial(tile_kernel, C, tiles, tile), out_shape=...  2.67 us

profile of v3, /device:TPU:0, one launch (start us, length us, event | category | flops | bytes accessed | tf_op | source)
XLA Modules:
  0.0 59.7 jit_solution(17278360462191513118)
XLA Ops:
  1.3 0.0 copy-start
  1.3 1.0 %copy-done = bf16[2048,128]{1,0:T(8,128)(2,1)S(1)} copy-done((bf16[2048,128]{1,0:T(8,128)(2,1)S(1)}, bf16[2048,128]{1,0:T(8,128)(2,1)}, u32[]{:S(2)}) %copy-start) | copy-done | bytes 524312
  2.3 0.0 copy-start.2
  2.3 1.2 %copy-done.2 = bf16[1,1,128,64,64]{2,4,3,1,0:T(8,128)(2,1)S(1)} copy-done((bf16[1,1,128,64,64]{2,4,3,1,0:T(8,128)(2,1)S(1)}, bf16[1,1,128,64,64]{2,4,3,1,0:T(8,128)(2,1)}, u32[]{:S(2)}) %copy-start.2) | copy-done | bytes 1048600
  3.5 0.0 copy-start.5
  3.6 0.7 %copy-done.5 = s32[1,1,128]{2,1,0:T(1,128)S(1)} copy-done((s32[1,1,128]{2,1,0:T(1,128)S(1)}, s32[1,1,128]{2,1,0:T(1,128)}, u32[]{:S(2)}) %copy-start.5) | copy-done | bytes 536
  4.2 0.0 copy-start.7
  4.2 22.8 %shard_map.103 = (bf16[2,2048,128]{2,1,0:T(8,128)(2,1)S(1)}, f32[2,32,64]{2,1,0:T(8,128)S(1)}, f32[32,64]{1,0:T(8,128)S(1)}, f32[4096,128]{1,0:T(8,128)S(1)}) custom-call(bf16[2048,128]{1,0:T(8,128)(2,1)S(1)} %copy-done, bf16[64,64,128]{2,1,0:T(8,128)(2,1)S(1)} %bitcast.11, s32[1,128]{1,0:T(1,128)S(1)} %bitcast.14, s32[1,1]{1,0:T(1,128)S(6)} %copy.14.live.count), custom_call_target="tpu_custom_call" | custom-call | tf_op jit(solution)/shard_map/pallas_call | solution.py:312
  27.1 0.0 copy-start.1
  27.1 0.0 copy-start.3
  27.1 0.0 copy-start.4
  27.1 0.0 copy-start.6
  27.1 0.7 %copy-done.6 = s32[1,1,128]{2,1,0:T(1,128)S(1)} copy-done((s32[1,1,128]{2,1,0:T(1,128)S(1)}, s32[1,1,128]{2,1,0:T(1,128)}, u32[]{:S(2)}) %copy-start.6) | copy-done | bytes 536
  27.8 2.7 %shard_map.104 = bf16[2048,128]{1,0:T(8,128)(2,1)S(1)} custom-call(s32[1,128]{1,0:T(1,128)S(1)} %bitcast.15, s32[1,128]{1,0:T(1,128)S(1)} %bitcast.16, s32[1,1]{1,0:T(1,128)S(6)} %copy.14.live.count, f32[4096,128]{1,0:T(8,128)S(1)} %get-tuple-element.10.values, bf16[2,2048,128]{2,1,0:T(8,128)(2,1)S(1)} %get-tuple-element.11.raw, ...), custom_call_target="tpu_custom_call" | custom-call | tf_op jit(solution)/shard_map/pallas_call | solution.py:326
  30.5 0.0 copy-done.7
  30.5 0.0 copy-done.1
  30.5 0.0 copy-done.3
  30.5 0.0 copy-done.4
  30.6 27.2 %shard_map.105 = (bf16[4,512,128]{2,1,0:T(8,128)(2,1)S(1)}, f32[4,32,128]{2,1,0:T(8,128)S(1)}, f32[1,128]{1,0:T(1,128)S(1)}) custom-call(bf16[4,512,128]{2,1,0:T(8,128)(2,1)S(1)} %bitcast.10, bf16[2048,128]{1,0:T(8,128)(2,1)S(1)} %copy-done.1, f32[32,64]{1,0:T(8,128)S(1)} %get-tuple-element.13.degree, bf16[2048,128]{1,0:T(8,128)(2,1)S(1)} %copy-done.3, ...), custom_call_target="tpu_custom_call" | custom-call | tf_op jit(solution)/shard_map/pallas_call | solution.py:337
  57.8 0.8 %copy.15 = bf16[2048,128]{1,0:T(8,128)(2,1)} copy(bf16[2048,128]{1,0:T(8,128)(2,1)S(1)} %bitcast.12) | data formatting | bytes 1048576
  58.6 0.6 %copy.16 = f32[128,128]{1,0:T(8,128)} copy(f32[128,128]{1,0:T(8,128)S(1)} %bitcast.13) | data formatting | bytes 131072
  59.2 0.5 copy.17
Async XLA Ops:
  1.3 1.0 %copy-start = (bf16[2048,128]{1,0:T(8,128)(2,1)S(1)}, bf16[2048,128]{1,0:T(8,128)(2,1)}, u32[]{:S(2)}) copy-start(bf16[2048,128]{1,0:T(8,128)(2,1)} %features.1) | copy-start | bytes 1572868
  2.3 1.2 %copy-start.2 = (bf16[1,1,128,64,64]{2,4,3,1,0:T(8,128)(2,1)S(1)}, bf16[1,1,128,64,64]{2,4,3,1,0:T(8,128)(2,1)}, u32[]{:S(2)}) copy-start(bf16[1,1,128,64,64]{2,4,3,1,0:T(8,128)(2,1)} %param.12) | copy-start | bytes 3145732
  3.5 0.7 %copy-start.5 = (s32[1,1,128]{2,1,0:T(1,128)S(1)}, s32[1,1,128]{2,1,0:T(1,128)}, u32[]{:S(2)}) copy-start(s32[1,1,128]{2,1,0:T(1,128)} %param.13) | copy-start | bytes 1540
  4.2 26.3 %copy-start.7 = (f32[128]{0:T(128)S(1)}, f32[128]{0:T(128)}, u32[]{:S(2)}) copy-start(f32[128]{0:T(128)} %param.10) | copy-start | bytes 1540
  27.1 3.5 %copy-start.1 = (bf16[2048,128]{1,0:T(8,128)(2,1)S(1)}, bf16[2048,128]{1,0:T(8,128)(2,1)}, u32[]{:S(2)}) copy-start(bf16[2048,128]{1,0:T(8,128)(2,1)} %features.1) | copy-start | bytes 1572868
  27.1 3.5 %copy-start.3 = (bf16[2048,128]{1,0:T(8,128)(2,1)S(1)}, bf16[2048,128]{1,0:T(8,128)(2,1)}, u32[]{:S(2)}) copy-start(bf16[2048,128]{1,0:T(8,128)(2,1)} %grad_out.1) | copy-start | bytes 1572868
  27.1 3.5 %copy-start.4 = (bf16[128,128]{1,0:T(8,128)(2,1)S(1)}, bf16[128,128]{1,0:T(8,128)(2,1)}, u32[]{:S(2)}) copy-start(bf16[128,128]{1,0:T(8,128)(2,1)} %weight.1) | copy-start | bytes 98308
  27.1 0.7 %copy-start.6 = (s32[1,1,128]{2,1,0:T(1,128)S(1)}, s32[1,1,128]{2,1,0:T(1,128)}, u32[]{:S(2)}) copy-start(s32[1,1,128]{2,1,0:T(1,128)} %param.14) | copy-start | bytes 1540

commit v4 on v3

--- a/solution.py
+++ b/solution.py
@@ -9,6 +9,7 @@
 MESH = pl.DeviceIdType.MESH
 CHUNKS = 16
 GROUP = 8
+PARTS = 4
 
 
 def spread_kernel(R, C, S, feat, stored, row_ids, live, buf, deg_x, deg_o, turned, values, fetched, deg_in, ldeg, send_f, recv_f, send_x, recv_x, send_o, recv_o):
@@ -222,30 +223,51 @@
             src_ref=dst.at[a], dst_ref=dst.at[a], send_sem=send.at[d], recv_sem=recv.at[a],
             device_id=(r, a), device_id_type=MESH)
 
-    for d in range(1, C):
-        to_rep(d, part.at[(j + d) % C], arrived, send_p, recv_p).start()
     q, feat_len = part.shape[1:]
+    step = q // PARTS
+
+    def to_owner(d, h):
+        rows = pl.ds(h * step, step)
+        return pltpu.make_async_remote_copy(
+            src_ref=part.at[(j + d) % C, rows], dst_ref=arrived.at[j, rows],
+            send_sem=send_p.at[d, h], recv_sem=recv_p.at[j, h],
+            device_id=(r, (j + d) % C), device_id_type=MESH)
+
+    for h in range(PARTS):
+        for d in range(1, C):
+            to_owner(d, h).start()
     tile = degree.shape[1]
-    mine_rows = pl.ds(pl.multiple_of(j * q, q), q)
     roots = lax.rsqrt(1.0 + degree[...].T)
     lane = lax.broadcasted_iota(jnp.int32, roots.shape, 1)
-    inv = jnp.concatenate([
+    inv_all = jnp.concatenate([
         jnp.broadcast_to(
             jnp.sum(jnp.where(lane == j * (q // tile) + a, roots, 0.0), axis=1, keepdims=True), (tile, feat_len))
         for a in range(q // tile)], axis=0)
-    scaled = (features[mine_rows].astype(jnp.float32) * inv).astype(jnp.bfloat16)
-    summed = part[j].astype(jnp.float32) + scaled.astype(jnp.float32)
-    for d in range(1, C):
-        from_rep(d, arrived, send_p, recv_p).wait_recv()
-        summed = summed + arrived[(j + d) % C].astype(jnp.float32)
-    smoothed = (inv * summed).astype(jnp.bfloat16)
-    preact = jnp.dot(smoothed, weight[...], preferred_element_type=jnp.float32) + bias[...]
-    sig = 1.0 / (1.0 + jnp.exp(-preact))
-    hidden[j] = (preact * sig).astype(jnp.bfloat16)
-    grad_pre = grad_out[mine_rows].astype(jnp.float32) * (sig * (1.0 + preact * (1.0 - sig)))
-    gb = jnp.sum(grad_pre, axis=0, keepdims=True)
-    gw = lax.dot_general(smoothed, grad_pre.astype(jnp.bfloat16), (((0,), (0,)), ((), ())),
-                         preferred_element_type=jnp.float32)
+    gb = jnp.zeros((1, feat_len), jnp.float32)
+    gw = jnp.zeros((feat_len, feat_len), jnp.float32)
+    for h in range(PARTS):
+        rows = slice(h * step, (h + 1) * step)
+        whole_rows = pl.ds(pl.multiple_of(j * q + h * step, step), step)
+        inv = inv_all[rows]
+        scaled = (features[whole_rows].astype(jnp.float32) * inv).astype(jnp.bfloat16)
+        summed = part[j, rows].astype(jnp.float32) + scaled.astype(jnp.float32)
+        for d in range(1, C):
+            a = (j + d) % C
+            place = pl.ds(h * step, step)
+            pltpu.make_async_remote_copy(
+                src_ref=arrived.at[a, place], dst_ref=arrived.at[a, place],
+                send_sem=send_p.at[d, h], recv_sem=recv_p.at[a, h],
+                device_id=(r, a), device_id_type=MESH).wait_recv()
+            summed = summed + arrived[a, rows].astype(jnp.float32)
+        smoothed = (inv * summed).astype(jnp.bfloat16)
+        preact = jnp.dot(smoothed, weight[...], preferred_element_type=jnp.float32) + bias[...]
+        sig = 1.0 / (1.0 + jnp.exp(-preact))
+        hidden[j, rows] = (preact * sig).astype(jnp.bfloat16)
+        grad_pre = grad_out[whole_rows].astype(jnp.float32) * (sig * (1.0 + preact * (1.0 - sig)))
+        gb = gb + jnp.sum(grad_pre, axis=0, keepdims=True)
+        gw = gw + lax.dot_general(
+            smoothed, grad_pre.astype(jnp.bfloat16), (((0,), (0,)), ((), ())),
+            preferred_element_type=jnp.float32)
     share = gw.shape[0] // C
     for a in range(C):
         g1[a, :share] = gw[a * share:(a + 1) * share]
@@ -286,7 +308,8 @@
         from_rep(d, grad_w, send_w, recv_w).wait_recv()
         from_rep(d, hidden, send_h, recv_h).wait_recv()
     for d in range(1, C):
-        to_rep(d, part.at[(j + d) % C], arrived, send_p, recv_p).wait_send()
+        for h in range(PARTS):
+            to_owner(d, h).wait_send()
         to_rep(d, hidden.at[j], hidden, send_h, recv_h).wait_send()
         to_rep(d, g1.at[(j + d) % C], g1_in, send_1, recv_1).wait_send()
         to_rep(d, grad_w.at[j], grad_w, send_w, recv_w).wait_send()
@@ -345,7 +368,7 @@
             pltpu.VMEM((C, share + 8, F), f32),
             pltpu.VMEM((R, share + 8, F), f32),
             pltpu.VMEM((share + 8, F), f32),
-            dma((C,)), dma((C,)), dma((C,)), dma((C,)), dma((C,)), dma((C,)), dma((R,)), dma((R,)),
+            dma((C, PARTS)), dma((C, PARTS)), dma((C,)), dma((C,)), dma((C,)), dma((C,)), dma((R,)), dma((R,)),
             dma((C,)), dma((C,))],
         compiler_params=pltpu.CompilerParams(
             collective_id=1, has_side_effects=True, vmem_limit_bytes=32 * 2**20),

time: 59.8 us -> 58.4 us (0.977)
  Pallas kernels: 52.7 us -> 50.9 us
    pallas_call x1, Pallas kernels: 27.2 us -> 25.8 us  [local(): pl.pallas_call(functools.partial(dense_kernel, R, C), out_shape=(sds((C,...]
where the time goes in v4:
time: 58.4 us; the launch traced here: 57.8 us
  Pallas kernels  50.9 us (87%)
  local copies, waits for them, and re-layouts  5.61 us (10%)
  between operations  1.38 us (2%)
    pallas_call x1, Pallas kernels, local(): pl.pallas_call(functools.partial(dense_kernel, R, C), out_shape=(sds((C,...  25.8 us
    pallas_call x1, Pallas kernels, local(): pl.pallas_call(functools.partial(spread_kernel, R, C, S), out_shape=(sds(...  22.8 us
    unnamed x19, local copies, waits for them, and re-layouts  5.61 us
    pallas_call x1, Pallas kernels, local(): pl.pallas_call(functools.partial(tile_kernel, C, tiles, tile), out_shape=...  2.19 us

profile of v4, /device:TPU:0, one launch (start us, length us, event | category | flops | bytes accessed | tf_op | source)
XLA Modules:
  0.0 57.8 jit_solution(5797440915857001678)
XLA Ops:
  1.3 0.0 copy-start
  1.3 1.0 %copy-done = bf16[2048,128]{1,0:T(8,128)(2,1)S(1)} copy-done((bf16[2048,128]{1,0:T(8,128)(2,1)S(1)}, bf16[2048,128]{1,0:T(8,128)(2,1)}, u32[]{:S(2)}) %copy-start) | copy-done | bytes 524312
  2.3 0.0 copy-start.2
  2.3 1.2 %copy-done.2 = bf16[1,1,128,64,64]{2,4,3,1,0:T(8,128)(2,1)S(1)} copy-done((bf16[1,1,128,64,64]{2,4,3,1,0:T(8,128)(2,1)S(1)}, bf16[1,1,128,64,64]{2,4,3,1,0:T(8,128)(2,1)}, u32[]{:S(2)}) %copy-start.2) | copy-done | bytes 1048600
  3.5 0.0 copy-start.5
  3.6 0.7 %copy-done.5 = s32[1,1,128]{2,1,0:T(1,128)S(1)} copy-done((s32[1,1,128]{2,1,0:T(1,128)S(1)}, s32[1,1,128]{2,1,0:T(1,128)}, u32[]{:S(2)}) %copy-start.5) | copy-done | bytes 536
  4.2 0.0 copy-start.7
  4.2 22.8 %shard_map.103 = (bf16[2,2048,128]{2,1,0:T(8,128)(2,1)S(1)}, f32[2,32,64]{2,1,0:T(8,128)S(1)}, f32[32,64]{1,0:T(8,128)S(1)}, f32[4096,128]{1,0:T(8,128)S(1)}) custom-call(bf16[2048,128]{1,0:T(8,128)(2,1)S(1)} %copy-done, bf16[64,64,128]{2,1,0:T(8,128)(2,1)S(1)} %bitcast.11, s32[1,128]{1,0:T(1,128)S(1)} %bitcast.14, s32[1,1]{1,0:T(1,128)S(6)} %copy.14.live.count), custom_call_target="tpu_custom_call" | custom-call | tf_op jit(solution)/shard_map/pallas_call | solution.py:335
  27.1 0.0 copy-start.1
  27.1 0.0 copy-start.3
  27.1 0.0 copy-start.4
  27.1 0.0 copy-start.6
  27.1 0.7 %copy-done.6 = s32[1,1,128]{2,1,0:T(1,128)S(1)} copy-done((s32[1,1,128]{2,1,0:T(1,128)S(1)}, s32[1,1,128]{2,1,0:T(1,128)}, u32[]{:S(2)}) %copy-start.6) | copy-done | bytes 536
  27.8 2.2 %shard_map.104 = bf16[2048,128]{1,0:T(8,128)(2,1)S(1)} custom-call(s32[1,128]{1,0:T(1,128)S(1)} %bitcast.15, s32[1,128]{1,0:T(1,128)S(1)} %bitcast.16, s32[1,1]{1,0:T(1,128)S(6)} %copy.14.live.count, f32[4096,128]{1,0:T(8,128)S(1)} %get-tuple-element.10.values, bf16[2,2048,128]{2,1,0:T(8,128)(2,1)S(1)} %get-tuple-element.11.raw, ...), custom_call_target="tpu_custom_call" | custom-call | tf_op jit(solution)/shard_map/pallas_call | solution.py:349
  30.0 0.0 copy-done.7
  30.0 0.0 copy-done.1
  30.1 0.0 copy-done.3
  30.1 0.0 copy-done.4
  30.1 25.8 %shard_map.105 = (bf16[4,512,128]{2,1,0:T(8,128)(2,1)S(1)}, f32[4,32,128]{2,1,0:T(8,128)S(1)}, f32[1,128]{1,0:T(1,128)S(1)}) custom-call(bf16[4,512,128]{2,1,0:T(8,128)(2,1)S(1)} %bitcast.10, bf16[2048,128]{1,0:T(8,128)(2,1)S(1)} %copy-done.1, f32[32,64]{1,0:T(8,128)S(1)} %get-tuple-element.13.degree, bf16[2048,128]{1,0:T(8,128)(2,1)S(1)} %copy-done.3, ...), custom_call_target="tpu_custom_call" | custom-call | tf_op jit(solution)/shard_map/pallas_call | solution.py:360
  55.9 0.8 %copy.15 = bf16[2048,128]{1,0:T(8,128)(2,1)} copy(bf16[2048,128]{1,0:T(8,128)(2,1)S(1)} %bitcast.12) | data formatting | bytes 1048576
  56.7 0.6 %copy.16 = f32[128,128]{1,0:T(8,128)} copy(f32[128,128]{1,0:T(8,128)S(1)} %bitcast.13) | data formatting | bytes 131072
  57.3 0.5 copy.17
Async XLA Ops:
  1.3 1.0 %copy-start = (bf16[2048,128]{1,0:T(8,128)(2,1)S(1)}, bf16[2048,128]{1,0:T(8,128)(2,1)}, u32[]{:S(2)}) copy-start(bf16[2048,128]{1,0:T(8,128)(2,1)} %features.1) | copy-start | bytes 1572868
  2.3 1.2 %copy-start.2 = (bf16[1,1,128,64,64]{2,4,3,1,0:T(8,128)(2,1)S(1)}, bf16[1,1,128,64,64]{2,4,3,1,0:T(8,128)(2,1)}, u32[]{:S(2)}) copy-start(bf16[1,1,128,64,64]{2,4,3,1,0:T(8,128)(2,1)} %param.12) | copy-start | bytes 3145732
  3.5 0.7 %copy-start.5 = (s32[1,1,128]{2,1,0:T(1,128)S(1)}, s32[1,1,128]{2,1,0:T(1,128)}, u32[]{:S(2)}) copy-start(s32[1,1,128]{2,1,0:T(1,128)} %param.13) | copy-start | bytes 1540
  4.2 25.8 %copy-start.7 = (f32[128]{0:T(128)S(1)}, f32[128]{0:T(128)}, u32[]{:S(2)}) copy-start(f32[128]{0:T(128)} %param.10) | copy-start | bytes 1540
  27.1 3.0 %copy-start.1 = (bf16[2048,128]{1,0:T(8,128)(2,1)S(1)}, bf16[2048,128]{1,0:T(8,128)(2,1)}, u32[]{:S(2)}) copy-start(bf16[2048,128]{1,0:T(8,128)(2,1)} %features.1) | copy-start | bytes 1572868
  27.1 3.0 %copy-start.3 = (bf16[2048,128]{1,0:T(8,128)(2,1)S(1)}, bf16[2048,128]{1,0:T(8,128)(2,1)}, u32[]{:S(2)}) copy-start(bf16[2048,128]{1,0:T(8,128)(2,1)} %grad_out.1) | copy-start | bytes 1572868
  27.1 3.0 %copy-start.4 = (bf16[128,128]{1,0:T(8,128)(2,1)S(1)}, bf16[128,128]{1,0:T(8,128)(2,1)}, u32[]{:S(2)}) copy-start(bf16[128,128]{1,0:T(8,128)(2,1)} %weight.1) | copy-start | bytes 98308
  27.1 0.7 %copy-start.6 = (s32[1,1,128]{2,1,0:T(1,128)S(1)}, s32[1,1,128]{2,1,0:T(1,128)}, u32[]{:S(2)}) copy-start(s32[1,1,128]{2,1,0:T(1,128)} %param.14) | copy-start | bytes 1540

commit v5 on v4

--- a/solution.py
+++ b/solution.py
@@ -8,7 +8,7 @@
 
 MESH = pl.DeviceIdType.MESH
 CHUNKS = 16
-GROUP = 8
+GROUP = 32
 PARTS = 4
 
 

time: 58.4 us -> 57.1 us (0.978)
  Pallas kernels: 50.9 us -> 49.7 us
    pallas_call x1, Pallas kernels: 25.8 us -> 25 us  [local(): pl.pallas_call(functools.partial(dense_kernel, R, C), out_shape=(sds((C,...]
where the time goes in v5:
time: 57.1 us; the launch traced here: 56.7 us
  Pallas kernels  49.7 us (87%)
  local copies, waits for them, and re-layouts  5.61 us (10%)
  between operations  1.38 us (2%)
    pallas_call x1, Pallas kernels, local(): pl.pallas_call(functools.partial(dense_kernel, R, C), out_shape=(sds((C,...  25 us
    pallas_call x1, Pallas kernels, local(): pl.pallas_call(functools.partial(spread_kernel, R, C, S), out_shape=(sds(...  22.8 us
    unnamed x19, local copies, waits for them, and re-layouts  5.61 us
    pallas_call x1, Pallas kernels, local(): pl.pallas_call(functools.partial(tile_kernel, C, tiles, tile), out_shape=...  1.92 us

profile of v5, /device:TPU:0, one launch (start us, length us, event | category | flops | bytes accessed | tf_op | source)
XLA Modules:
  0.0 56.7 jit_solution(13306064126199926800)
XLA Ops:
  1.3 0.0 copy-start
  1.3 1.0 %copy-done = bf16[2048,128]{1,0:T(8,128)(2,1)S(1)} copy-done((bf16[2048,128]{1,0:T(8,128)(2,1)S(1)}, bf16[2048,128]{1,0:T(8,128)(2,1)}, u32[]{:S(2)}) %copy-start) | copy-done | bytes 524312
  2.3 0.0 copy-start.2
  2.3 1.2 %copy-done.2 = bf16[1,1,128,64,64]{2,4,3,1,0:T(8,128)(2,1)S(1)} copy-done((bf16[1,1,128,64,64]{2,4,3,1,0:T(8,128)(2,1)S(1)}, bf16[1,1,128,64,64]{2,4,3,1,0:T(8,128)(2,1)}, u32[]{:S(2)}) %copy-start.2) | copy-done | bytes 1048600
  3.5 0.0 copy-start.5
  3.6 0.7 %copy-done.5 = s32[1,1,128]{2,1,0:T(1,128)S(1)} copy-done((s32[1,1,128]{2,1,0:T(1,128)S(1)}, s32[1,1,128]{2,1,0:T(1,128)}, u32[]{:S(2)}) %copy-start.5) | copy-done | bytes 536
  4.2 0.0 copy-start.7
  4.2 22.8 %shard_map.103 = (bf16[2,2048,128]{2,1,0:T(8,128)(2,1)S(1)}, f32[2,32,64]{2,1,0:T(8,128)S(1)}, f32[32,64]{1,0:T(8,128)S(1)}, f32[4096,128]{1,0:T(8,128)S(1)}) custom-call(bf16[2048,128]{1,0:T(8,128)(2,1)S(1)} %copy-done, bf16[64,64,128]{2,1,0:T(8,128)(2,1)S(1)} %bitcast.11, s32[1,128]{1,0:T(1,128)S(1)} %bitcast.14, s32[1,1]{1,0:T(1,128)S(6)} %copy.14.live.count), custom_call_target="tpu_custom_call" | custom-call | tf_op jit(solution)/shard_map/pallas_call | solution.py:335
  27.1 0.0 copy-start.1
  27.1 0.0 copy-start.3
  27.1 0.0 copy-start.4
  27.1 0.0 copy-start.6
  27.1 0.7 %copy-done.6 = s32[1,1,128]{2,1,0:T(1,128)S(1)} copy-done((s32[1,1,128]{2,1,0:T(1,128)S(1)}, s32[1,1,128]{2,1,0:T(1,128)}, u32[]{:S(2)}) %copy-start.6) | copy-done | bytes 536
  27.8 1.9 %shard_map.104 = bf16[2048,128]{1,0:T(8,128)(2,1)S(1)} custom-call(s32[1,128]{1,0:T(1,128)S(1)} %bitcast.15, s32[1,128]{1,0:T(1,128)S(1)} %bitcast.16, s32[1,1]{1,0:T(1,128)S(6)} %copy.14.live.count, f32[4096,128]{1,0:T(8,128)S(1)} %get-tuple-element.10.values, bf16[2,2048,128]{2,1,0:T(8,128)(2,1)S(1)} %get-tuple-element.11.raw, ...), custom_call_target="tpu_custom_call" | custom-call | tf_op jit(solution)/shard_map/pallas_call | solution.py:349
  29.8 0.0 copy-done.7
  29.8 0.0 copy-done.1
  29.8 0.0 copy-done.3
  29.8 0.0 copy-done.4
  29.8 25.0 %shard_map.105 = (bf16[4,512,128]{2,1,0:T(8,128)(2,1)S(1)}, f32[4,32,128]{2,1,0:T(8,128)S(1)}, f32[1,128]{1,0:T(1,128)S(1)}) custom-call(bf16[4,512,128]{2,1,0:T(8,128)(2,1)S(1)} %bitcast.10, bf16[2048,128]{1,0:T(8,128)(2,1)S(1)} %copy-done.1, f32[32,64]{1,0:T(8,128)S(1)} %get-tuple-element.13.degree, bf16[2048,128]{1,0:T(8,128)(2,1)S(1)} %copy-done.3, ...), custom_call_target="tpu_custom_call" | custom-call | tf_op jit(solution)/shard_map/pallas_call | solution.py:360
  54.8 0.8 %copy.15 = bf16[2048,128]{1,0:T(8,128)(2,1)} copy(bf16[2048,128]{1,0:T(8,128)(2,1)S(1)} %bitcast.12) | data formatting | bytes 1048576
  55.6 0.6 %copy.16 = f32[128,128]{1,0:T(8,128)} copy(f32[128,128]{1,0:T(8,128)S(1)} %bitcast.13) | data formatting | bytes 131072
  56.2 0.5 copy.17
Async XLA Ops:
  1.3 1.0 %copy-start = (bf16[2048,128]{1,0:T(8,128)(2,1)S(1)}, bf16[2048,128]{1,0:T(8,128)(2,1)}, u32[]{:S(2)}) copy-start(bf16[2048,128]{1,0:T(8,128)(2,1)} %features.1) | copy-start | bytes 1572868
  2.3 1.2 %copy-start.2 = (bf16[1,1,128,64,64]{2,4,3,1,0:T(8,128)(2,1)S(1)}, bf16[1,1,128,64,64]{2,4,3,1,0:T(8,128)(2,1)}, u32[]{:S(2)}) copy-start(bf16[1,1,128,64,64]{2,4,3,1,0:T(8,128)(2,1)} %param.12) | copy-start | bytes 3145732
  3.5 0.7 %copy-start.5 = (s32[1,1,128]{2,1,0:T(1,128)S(1)}, s32[1,1,128]{2,1,0:T(1,128)}, u32[]{:S(2)}) copy-start(s32[1,1,128]{2,1,0:T(1,128)} %param.13) | copy-start | bytes 1540
  4.2 25.6 %copy-start.7 = (f32[128]{0:T(128)S(1)}, f32[128]{0:T(128)}, u32[]{:S(2)}) copy-start(f32[128]{0:T(128)} %param.10) | copy-start | bytes 1540
  27.1 2.7 %copy-start.1 = (bf16[2048,128]{1,0:T(8,128)(2,1)S(1)}, bf16[2048,128]{1,0:T(8,128)(2,1)}, u32[]{:S(2)}) copy-start(bf16[2048,128]{1,0:T(8,128)(2,1)} %features.1) | copy-start | bytes 1572868
  27.1 2.7 %copy-start.3 = (bf16[2048,128]{1,0:T(8,128)(2,1)S(1)}, bf16[2048,128]{1,0:T(8,128)(2,1)}, u32[]{:S(2)}) copy-start(bf16[2048,128]{1,0:T(8,128)(2,1)} %grad_out.1) | copy-start | bytes 1572868
  27.1 2.7 %copy-start.4 = (bf16[128,128]{1,0:T(8,128)(2,1)S(1)}, bf16[128,128]{1,0:T(8,128)(2,1)}, u32[]{:S(2)}) copy-start(bf16[128,128]{1,0:T(8,128)(2,1)} %weight.1) | copy-start | bytes 98308
  27.1 0.7 %copy-start.6 = (s32[1,1,128]{2,1,0:T(1,128)S(1)}, s32[1,1,128]{2,1,0:T(1,128)}, u32[]{:S(2)}) copy-start(s32[1,1,128]{2,1,0:T(1,128)} %param.14) | copy-start | bytes 1540
